TPU v7x, 256 devices: a whole 4x4x8 slice. The times are simulated.
256 devices in a mesh: dom: 16 (over y_hi, x, core), space: 16 (over y_lo, z).
Axes of the slice: x: 4, y: 4 (y_hi: 2, y_lo: 2; y = y_hi * 2 + y_lo), z: 8, core: 2. Of those that a mesh axis runs over, the one named last changes fastest.
Arguments:
- ensemble: float32 [512, 4, 16, 8192], P('dom', None, None, 'space'), may hold values from -6 to 6
- ancestors: int32 [512], replicated, may hold values from 0 to 511, as said below
- perturbation: float32 [512, 16, 8192], P('dom', None, 'space'), may hold values from -4 to 4
- levels: int32 [16, 8192], P(None, 'space'), may hold values from 0 to 3
- observed: float32 [16, 8192], P(None, 'space'), may hold values from -6 to 6
Outputs:
- forecast: float32 [512, 4, 16, 8192], P('dom', None, None, 'space')
Inputs may be any that keep to these rules, and one draw needn't show every extreme that they name: `ancestors`: call slots and particles k*32 to k*32 + 31 block k. In every block k after the first, the first 2 slots copy the last 2 particles of block k-1, each exactly once; in every block k before the last, the last 2 slots copy the first 2 particles of block k+1, each exactly once; every other slot copies a particle of its own block.
All inputs are finite; a program needn't handle non-finite values.
Results may differ from a plain program's by a relative error of at most 0.00012.
Values sent between devices are 32-bit elements; how exact they have to be, the bound alone decides.
A program may use at most 64 MiB of HBM per device.

v0:
```python
import functools

import jax
import jax.numpy as jnp
from jax import lax
from jax.experimental import pallas as pl
from jax.experimental.pallas import tpu as pltpu
from jax.sharding import PartitionSpec as P

MESH = pl.DeviceIdType.MESH
STEPS = 3
CAP = 2
EDGE = 2 * STEPS
LANES = 128
TOP = 8
PITCH = 32
UNIT = 4
E_, N_, H_, C_ = range(4)


def lane_of(shape):
    return lax.broadcasted_iota(jnp.int32, shape, len(shape) - 1)


def east(cells, joined):
    turned = pltpu.roll(cells, LANES - 1, 2)
    if not joined:
        return turned
    following = jnp.concatenate([turned[1:], turned[:1]], axis=0)
    return jnp.where(lane_of(cells.shape) == LANES - 1, following, turned)


def west(cells, joined):
    turned = pltpu.roll(cells, 1, 2)
    if not joined:
        return turned
    preceding = jnp.concatenate([turned[-1:], turned[:-1]], axis=0)
    return jnp.where(lane_of(cells.shape) == 0, preceding, turned)


def flow(read, wet, turn, joined):
    e, n, h = read(E_, 0), read(N_, 0), read(H_, 0)
    e_new = wet * (
        (5.5 * e + turn * n)
        + (read(E_, 1) + read(E_, -1))
        + (east(e - h, joined) + west(e + h, joined))
    )
    n_new = wet * (
        (5.5 * n - turn * e)
        + (east(n, joined) + west(n, joined))
        + ((read(N_, 1) - read(H_, 1)) + (read(N_, -1) + read(H_, -1)))
    )
    return e_new, n_new


def level(read, read_new, depth, pull, last, joined):
    e, n = read_new(E_, 0), read_new(N_, 0)
    spread = (east(e, joined) - west(e, joined)) + (read_new(N_, 1) - read_new(N_, -1))
    h_new = ((0.18 if last else 0.9) * read(H_, 0) + pull) - depth * spread
    c = read(C_, 0)
    c_east, c_west = east(c, joined), west(c, joined)
    c_north, c_south = read(C_, 1), read(C_, -1)
    c_new = (
        (6.0 * c + ((c_east + c_west) + (c_north + c_south)))
        - e * (c_east - c_west)
        - n * (c_north - c_south)
    )
    if last:
        c_new = 0.001 * c_new
    return h_new, c_new


def kernel(
    anc, ens, pert, lev, obs, out,
    own, ext, h0, pv, lv, ov, gw, gd, go, s1, s2,
    out1, out2, in1, in2, gs, b0, b1, b2,
    in_sem, dom_out_sem, dom_in_sem, msg_out_sem, msg_in_sem,
):
    pd = ens.shape[0]
    ny = ens.shape[2]
    tiles = ens.shape[3] // LANES
    doms, spaces = lax.axis_size("dom"), lax.axis_size("space")
    k, me = lax.axis_index("dom"), lax.axis_index("space")
    prev_space, next_space = lax.rem(me + spaces - 1, spaces), lax.rem(me + 1, spaces)
    prev_dom, next_dom = lax.rem(k + doms - 1, doms), lax.rem(k + 1, doms)
    early = pd - 2 * CAP
    rows = slice(TOP, TOP + ny)

    barrier = pltpu.get_barrier_semaphore()
    for where in ((k, prev_space), (k, next_space), (prev_dom, me), (next_dom, me)):
        pl.semaphore_signal(barrier, inc=1, device_id=where, device_id_type=MESH)

    def tile(q):
        return pl.ds(q * LANES, LANES)

    loads = []
    for q in range(tiles):
        loads.append(pltpu.make_async_copy(lev.at[:, tile(q)], lv.at[q], in_sem.at[0, q]))
        loads.append(pltpu.make_async_copy(obs.at[:, tile(q)], ov.at[q], in_sem.at[1, q]))
        loads.append(pltpu.make_async_copy(pert.at[:, :, tile(q)], pv.at[:, q], in_sem.at[2, q]))
        loads.append(pltpu.make_async_copy(ens.at[:, :, :, tile(q)], own.at[:, :, q, rows], in_sem.at[3, q]))
    for copy in loads:
        copy.start()

    pl.semaphore_wait(barrier, 4)

    def dom_copy(up, q):
        first, lands, to = (pd - CAP, 0, next_dom) if up else (0, CAP, prev_dom)
        return pltpu.make_async_remote_copy(
            src_ref=ens.at[first : first + CAP, :, :, tile(q)],
            dst_ref=ext.at[lands : lands + CAP, :, q, rows],
            send_sem=dom_out_sem.at[int(up), q],
            recv_sem=dom_in_sem.at[int(up), q],
            device_id=(to, me),
            device_id_type=MESH,
        )

    @pl.when(k < doms - 1)
    def _():
        for q in range(tiles):
            dom_copy(True, q).start()

    @pl.when(k > 0)
    def _():
        for q in range(tiles):
            dom_copy(False, q).start()

    def clear(ref, count):
        @pl.loop(0, count)
        def _(i):
            blank = jnp.zeros(ref.shape[1:-2] + (8, LANES), jnp.float32)
            ref[i, ..., TOP - 8 : TOP, :] = blank
            ref[i, ..., TOP + ny : TOP + ny + 8, :] = blank

    clear(own, pd)
    clear(ext, 2 * CAP)
    clear(h0, pd)
    for ref in (s1, s2, b0, b1, b2):
        clear(ref, ref.shape[0])

    for copy in loads:
        copy.wait()

    y_of = lax.broadcasted_iota(jnp.int32, (1, ny, LANES), 1).astype(jnp.float32)
    turn = 2.0 * (0.2 + 0.6 * y_of / ny)

    def ground(levels, observed, wet_ref, depth_ref, pull_ref):
        wet_ref[...] = jnp.where(levels > 0, 0.1, 0.0).astype(jnp.float32)
        depth_ref[0] = 1.25 * levels
        depth_ref[1] = 0.25 * levels
        pull_ref[0] = 0.5 * observed
        pull_ref[1] = 0.1 * observed

    ground(lv[...].astype(jnp.float32), ov[...], gw, gd, go)

    def from_own(j):
        return jnp.clip(anc[k * pd + j] - k * pd, 0, pd - 1)

    def from_ext(j, low):
        parent = anc[k * pd + j]
        if low:
            return jnp.where(k == 0, j, jnp.clip(parent - (k * pd - CAP), 0, CAP - 1))
        return jnp.where(
            k == doms - 1, j - (pd - 2 * CAP), jnp.clip(parent - (k + 1) * pd, 0, CAP - 1) + CAP
        )

    @pl.loop(CAP, pd - CAP)
    def _(j):
        h0[j, :, rows] = 5.0 * (own[from_own(j), H_, :, rows] + pv[j])

    def column(ref, i, j, q):
        return jnp.concatenate(
            [ref[i, E_ : N_ + 1, q, rows], h0[j, q, rows][None], ref[i, C_:, q, rows]], axis=0
        )

    lane = lane_of((1, 1, LANES))
    half = lax.rem(lane, 64)

    def packed(ref, i, j, at, to_left, to_right):
        chosen = (lane >= at) & (lane < at + EDGE)
        to_left = jnp.where(chosen, pltpu.roll(column(ref, i, j, 0), at, 2), to_left)
        to_right = jnp.where(chosen, pltpu.roll(column(ref, i, j, tiles - 1), at + EDGE, 2), to_right)
        return to_left, to_right

    def message(second, rightward):
        src, dst = (out2, in2) if second else (out1, in1)
        return pltpu.make_async_remote_copy(
            src_ref=src.at[int(rightward)],
            dst_ref=dst.at[int(rightward)],
            send_sem=msg_out_sem.at[int(second), int(rightward)],
            recv_sem=msg_in_sem.at[int(second), int(rightward)],
            device_id=(k, next_space if rightward else prev_space),
            device_id_type=MESH,
        )

    blank = jnp.zeros((4, ny, LANES), jnp.float32)
    for m, pairs in enumerate((8, (early - 16) // 2)):

        def pack(p, carry):
            for s in range(2):
                j = CAP + 16 * m + 2 * p + s
                carry = packed(own, from_own(j), j, 64 * s + 8 * p, *carry)
            return carry

        left, right = lax.fori_loop(0, pairs, pack, (blank, blank))
        out1[0, 4 * m : 4 * m + 4] = left
        out1[1, 4 * m : 4 * m + 4] = right
    for i, field in enumerate((lv[...].astype(jnp.float32), ov[...])):
        out1[0, 8 + i] = jnp.where(half < EDGE, jnp.where(lane < 64, field[:1], pltpu.roll(field[:1], 64, 2)), 0.0)[0]
        end = field[tiles - 1 :]
        out1[1, 8 + i] = jnp.where(
            half < EDGE, jnp.where(lane < 64, pltpu.roll(end, EDGE, 2), pltpu.roll(end, 64 + EDGE, 2)), 0.0
        )[0]
    message(False, False).start()
    message(False, True).start()

    def unit(slots, src, where):
        for step in range(STEPS):
            last = step == STEPS - 1
            old, new = (None, s1) if step == 0 else (s1, s2) if step == 1 else (s2, s1)
            now = pl.ds(TOP, ny)

            def reader(ref, s):
                return lambda field, up: ref[s, field, :, pl.ds(TOP + up, ny)]

            def first_reader(s):
                return lambda field, up: (
                    h0[slots[s], :, pl.ds(TOP + up, ny)]
                    if field == H_
                    else src[where[s], field, :, pl.ds(TOP + up, ny)]
                )

            read = [first_reader(s) if step == 0 else reader(old, s) for s in range(UNIT)]
            for s in range(UNIT):
                e, n = flow(read[s], gw[...], turn, True)
                new[s, E_, :, now] = e
                new[s, N_, :, now] = n
                if last:
                    out[slots[s], E_] = e
                    out[slots[s], N_] = n
            for s in range(UNIT):
                h, c = level(read[s], reader(new, s), gd[int(last)], go[int(last)], last, True)
                if last:
                    out[slots[s], H_] = h
                    out[slots[s], C_] = c
                else:
                    new[s, H_, :, now] = h
                    new[s, C_, :, now] = c

    @pl.loop(0, early // UNIT)
    def _(i):
        slots = [CAP + i * UNIT + s for s in range(UNIT)]
        unit(slots, own, [from_own(j) for j in slots])

    late = [0, 1, pd - 2, pd - 1]

    @pl.when(k > 0)
    def _():
        for q in range(tiles):
            dom_copy(True, q).wait_recv()

    @pl.when(k < doms - 1)
    def _():
        for q in range(tiles):
            dom_copy(False, q).wait_recv()

    @pl.when(k == 0)
    def _():
        for s in range(CAP):
            ext[s, :, :, rows] = own[from_own(late[s]), :, :, rows]

    @pl.when(k == doms - 1)
    def _():
        for s in range(CAP, 2 * CAP):
            ext[s, :, :, rows] = own[from_own(late[s]), :, :, rows]

    late_from = [from_ext(j, j < CAP) for j in late]
    left, right = blank, blank
    for t, j in enumerate(late):
        h0[j, :, rows] = 5.0 * (ext[late_from[t], H_, :, rows] + pv[j])
    for t, j in enumerate(late):
        left, right = packed(ext, late_from[t], j, 64 * (t % 2) + 8 * (t // 2), left, right)
    out2[0] = left
    out2[1] = right
    message(True, False).start()
    message(True, True).start()
    unit(late, ext, late_from)

    message(False, False).wait_recv()
    message(False, True).wait_recv()

    def ends(first, final, s, tile_so_far):
        base = 64 * s
        inner = (lane >= base + EDGE) & (lane < base + 3 * EDGE)
        tile_so_far = jnp.where(inner, pltpu.roll(first, base + EDGE, 2), tile_so_far)
        inner = (lane >= base + 32) & (lane < base + 32 + 2 * EDGE)
        return jnp.where(inner, pltpu.roll(final, (base + 32 + 2 * EDGE) % LANES, 2), tile_so_far)

    def beyond(from_left, from_right, p):
        shift_left = (LANES - 8 * p) % LANES if isinstance(p, int) else lax.rem(LANES - 8 * p, LANES)
        shift_right = (LANES + 44 - 8 * p) % LANES if isinstance(p, int) else lax.rem(LANES + 44 - 8 * p, LANES)
        got = jnp.where(half < EDGE, pltpu.roll(from_left, shift_left, 2), 0.0)
        return jnp.where((half >= 44) & (half < 44 + EDGE), pltpu.roll(from_right, shift_right, 2), got)

    fields = []
    for i, field in enumerate((lv[...].astype(jnp.float32), ov[...])):
        got = beyond(in1[1, 8 + i][None], in1[0, 8 + i][None], 0)
        for s in range(2):
            got = ends(field[:1], field[tiles - 1 :], s, got)
        fields.append(got[0])
    gs[0] = jnp.where(fields[0] > 0, 0.1, 0.0).astype(jnp.float32)
    gs[1] = 1.25 * fields[0]
    gs[2] = 0.25 * fields[0]
    gs[3] = 0.5 * fields[1]
    gs[4] = 0.1 * fields[1]

    def strips(chunk_pairs):
        now = pl.ds(TOP, ny)
        for p, (got, slots) in enumerate(chunk_pairs):
            for s, (src, where, j) in enumerate(slots):
                got = ends(column(src, where, j, 0), column(src, where, j, tiles - 1), s, got)
            b0[:, p, now] = got

        def reader(ref):
            return lambda field, up: ref[field, :, pl.ds(TOP + up, ny)]

        for step in range(STEPS):
            last = step == STEPS - 1
            old, new = ((b0, b1), (b1, b2), (b2, b0))[step]
            e, n = flow(reader(old), gs[0][None], turn, False)
            new[E_, :, now] = e
            new[N_, :, now] = n
            depth, pull = (gs[2], gs[4]) if last else (gs[1], gs[3])
            h, c = level(reader(old), reader(new), depth[None], pull[None], last, False)
            new[H_, :, now] = h
            new[C_, :, now] = c
        for p, (_, slots) in enumerate(chunk_pairs):
            done = b0[:, p, now]
            for s, (_, _, j) in enumerate(slots):
                base = 64 * s
                at_left = pltpu.roll(done, LANES - EDGE - base, 2)
                at_right = pltpu.roll(done, (LANES - EDGE - (base + 32 + EDGE)) % LANES, 2)
                on = jnp.broadcast_to(lane < EDGE, done.shape)
                pltpu.store(out.at[j, :, 0], at_left, mask=on)
                on = jnp.broadcast_to(lane >= LANES - EDGE, done.shape)
                pltpu.store(out.at[j, :, tiles - 1], at_right, mask=on)

    def early_pair(m, p_in_message, first_slot):
        got = beyond(in1[1, pl.ds(4 * m, 4)], in1[0, pl.ds(4 * m, 4)], p_in_message)
        return got, [(own, from_own(first_slot + s), first_slot + s) for s in range(2)]

    @pl.loop(0, early // 8)
    def _(c):
        strips([early_pair(c // 2, 4 * lax.rem(c, 2) + p, CAP + 8 * c + 2 * p) for p in range(4)])

    message(True, False).wait_recv()
    message(True, True).wait_recv()
    done = early // 8 * 8
    mixed = [early_pair(1, (done - 16) // 2 + p, CAP + done + 2 * p) for p in range(2)]
    for p in range(2):
        got = beyond(in2[1], in2[0], p)
        mixed.append((got, [(ext, late_from[2 * p + s], late[2 * p + s]) for s in range(2)]))
    strips(mixed)

    for second in (False, True):
        for rightward in (False, True):
            message(second, rightward).wait_send()

    @pl.when(k < doms - 1)
    def _():
        for q in range(tiles):
            dom_copy(True, q).wait_send()

    @pl.when(k > 0)
    def _():
        for q in range(tiles):
            dom_copy(False, q).wait_send()


def put_out(made, out, sem):
    copies = [
        pltpu.make_async_copy(made.at[:, :, q], out.at[:, :, :, pl.ds(q * LANES, LANES)], sem.at[q])
        for q in range(made.shape[2])
    ]
    for copy in copies:
        copy.start()
    for copy in copies:
        copy.wait()


def local(ensemble, ancestors, perturbation, levels, observed):
    pd, nf, ny, nx = ensemble.shape
    tiles = nx // LANES
    f32 = jnp.float32
    hbm = pl.BlockSpec(memory_space=pltpu.HBM)
    made = pl.pallas_call(
        kernel,
        out_shape=pltpu.VMEM((pd, nf, tiles, ny, LANES), f32),
        in_specs=[pl.BlockSpec(memory_space=pltpu.SMEM), hbm, hbm, hbm, hbm],
        out_specs=pl.BlockSpec(memory_space=pltpu.VMEM),
        scratch_shapes=[
            pltpu.VMEM((pd, nf, tiles, PITCH, LANES), f32),
            pltpu.VMEM((2 * CAP, nf, tiles, PITCH, LANES), f32),
            pltpu.VMEM((pd, tiles, PITCH, LANES), f32),
            pltpu.VMEM((pd, tiles, ny, LANES), f32),
            pltpu.VMEM((tiles, ny, LANES), jnp.int32),
            pltpu.VMEM((tiles, ny, LANES), f32),
            pltpu.VMEM((tiles, ny, LANES), f32),
            pltpu.VMEM((2, tiles, ny, LANES), f32),
            pltpu.VMEM((2, tiles, ny, LANES), f32),
            pltpu.VMEM((UNIT, nf, tiles, PITCH, LANES), f32),
            pltpu.VMEM((UNIT, nf, tiles, PITCH, LANES), f32),
            pltpu.VMEM((2, 10, ny, LANES), f32),
            pltpu.VMEM((2, nf, ny, LANES), f32),
            pltpu.VMEM((2, 10, ny, LANES), f32),
            pltpu.VMEM((2, nf, ny, LANES), f32),
            pltpu.VMEM((5, ny, LANES), f32),
            pltpu.VMEM((nf, 4, PITCH, LANES), f32),
            pltpu.VMEM((nf, 4, PITCH, LANES), f32),
            pltpu.VMEM((nf, 4, PITCH, LANES), f32),
            pltpu.SemaphoreType.DMA((4, tiles)),
            pltpu.SemaphoreType.DMA((2, tiles)),
            pltpu.SemaphoreType.DMA((2, tiles)),
            pltpu.SemaphoreType.DMA((2, 2)),
            pltpu.SemaphoreType.DMA((2, 2)),
        ],
        compiler_params=pltpu.CompilerParams(
            collective_id=0, has_side_effects=True, vmem_limit_bytes=40 * 1024 * 1024
        ),
        name="resample_and_step",
    )(*(pltpu.with_memory_space_constraint(x, pltpu.HBM) for x in (ancestors, ensemble, perturbation, levels, observed)))
    return pl.pallas_call(
        put_out,
        out_shape=jax.ShapeDtypeStruct((pd, nf, ny, nx), f32),
        in_specs=[pl.BlockSpec(memory_space=pltpu.VMEM)],
        out_specs=hbm,
        scratch_shapes=[pltpu.SemaphoreType.DMA((tiles,))],
        compiler_params=pltpu.CompilerParams(vmem_limit_bytes=16 * 1024 * 1024),
        name="put_out",
    )(made)


def solution(mesh):
    return jax.shard_map(
        local,
        mesh=mesh,
        in_specs=(
            P("dom", None, None, "space"),
            P(),
            P("dom", None, "space"),
            P(None, "space"),
            P(None, "space"),
        ),
        out_specs=P("dom", None, None, "space"),
        check_vma=False,
    )
```

profile of v0, /device:TPU:8, one launch (start us, length us, event | category | flops | bytes accessed | tf_op | source)
XLA Modules:
  0.0 25.7 jit_solution(8713802142846529639)
XLA Ops:
  0.0 23.6 %resample_and_step.1.made = f32[32,4,4,16,128]{4,3,2,1,0:T(8,128)S(1)} custom-call(s32[512]{0:T(512)} %anc.1, f32[32,4,16,512]{3,2,1,0:T(8,128)} %ens.1, f32[32,16,512]{2,1,0:T(8,128)} %pert.1, s32[16,512]{1,0:T(8,128)} %lev.1, f32[16,512]{1,0:T(8,128)} %obs.1), custom_call_target="tpu_custom_call" | custom-call | tf_op jit(solution)/shard_map/resample_and_step/pallas_call | solution.py:396
  23.6 2.0 %put_out.1 = f32[32,4,16,512]{3,2,1,0:T(8,128)} custom-call(f32[32,4,4,16,128]{4,3,2,1,0:T(8,128)S(1)} %resample_and_step.1.made), custom_call_target="tpu_custom_call" | custom-call | tf_op jit(solution)/shard_map/put_out/pallas_call | solution.py:432
where the time goes:
time: 25.8 us; the launch traced here: 25.7 us
  Pallas kernels  25.7 us (100%)
    pallas_call x1, Pallas kernels, local(): pl.pallas_call(kernel, out_shape=pltpu.VMEM((pd, nf, tiles, ny, LANES), f...  23.6 us
    pallas_call x1, Pallas kernels, local(): pl.pallas_call(put_out, out_shape=jax.ShapeDtypeStruct((pd, nf, ny, nx),...  2.04 us

commit v1 on v0

v1 whole, which is shorter than its diff:
```python
import functools

import jax
import jax.numpy as jnp
from jax import lax
from jax.experimental import pallas as pl
from jax.experimental.pallas import tpu as pltpu
from jax.sharding import PartitionSpec as P

MESH = pl.DeviceIdType.MESH
STEPS = 3
CAP = 2
EDGE = 2 * STEPS
LANES = 128
TOP = 8
PITCH = 32
UNIT = 4
HALF = 8
E_, N_, H_, C_ = range(4)


def lane_of(shape):
    return lax.broadcasted_iota(jnp.int32, shape, len(shape) - 1)


def east(cells, joined):
    turned = pltpu.roll(cells, LANES - 1, 2)
    if not joined:
        return turned
    following = jnp.concatenate([turned[1:], turned[:1]], axis=0)
    return jnp.where(lane_of(cells.shape) == LANES - 1, following, turned)


def west(cells, joined):
    turned = pltpu.roll(cells, 1, 2)
    if not joined:
        return turned
    preceding = jnp.concatenate([turned[-1:], turned[:-1]], axis=0)
    return jnp.where(lane_of(cells.shape) == 0, preceding, turned)


def flow(read, wet, turn, joined):
    e, n, h = read(E_, 0), read(N_, 0), read(H_, 0)
    e_new = wet * (
        (5.5 * e + turn * n)
        + (read(E_, 1) + read(E_, -1))
        + (east(e - h, joined) + west(e + h, joined))
    )
    n_new = wet * (
        (5.5 * n - turn * e)
        + (east(n, joined) + west(n, joined))
        + ((read(N_, 1) - read(H_, 1)) + (read(N_, -1) + read(H_, -1)))
    )
    return e_new, n_new


def level(read, read_new, depth, pull, last, joined):
    e, n = read_new(E_, 0), read_new(N_, 0)
    spread = (east(e, joined) - west(e, joined)) + (read_new(N_, 1) - read_new(N_, -1))
    h_new = ((0.18 if last else 0.9) * read(H_, 0) + pull) - depth * spread
    c = read(C_, 0)
    c_east, c_west = east(c, joined), west(c, joined)
    c_north, c_south = read(C_, 1), read(C_, -1)
    c_new = (
        (6.0 * c + ((c_east + c_west) + (c_north + c_south)))
        - e * (c_east - c_west)
        - n * (c_north - c_south)
    )
    if last:
        c_new = 0.001 * c_new
    return h_new, c_new


def level_of(levels, observed):
    return (
        jnp.where(levels > 0, 0.1, 0.0).astype(jnp.float32),
        1.25 * levels,
        0.25 * levels,
        0.5 * observed,
        0.1 * observed,
    )


def turn_of(ny, y0):
    y = lax.broadcasted_iota(jnp.int32, (1, HALF, LANES), 1).astype(jnp.float32) + float(y0)
    return 2.0 * (0.2 + 0.6 * y / ny)


def kernel(
    anc, ens, pert, lev, obs, out, b0, gs,
    own, ext, h0, pv, lv, ov, gw, gd, go, s1, s2, out1, in1, edge_out, edge_in,
    in_sem, dom_out_sem, dom_in_sem, msg_out_sem, msg_in_sem, edge_out_sem, edge_in_sem,
):
    pd = ens.shape[0]
    ny = ens.shape[2]
    tiles = ens.shape[3] // LANES
    doms, spaces = lax.axis_size("dom"), lax.axis_size("space")
    k, me = lax.axis_index("dom"), lax.axis_index("space")
    prev_space, next_space = lax.rem(me + spaces - 1, spaces), lax.rem(me + 1, spaces)
    early = pd - 2 * CAP
    rows = slice(TOP, TOP + ny)

    barrier = pltpu.get_barrier_semaphore()


    def greet(dom, *spaces_there):
        for space in spaces_there:
            pl.semaphore_signal(barrier, inc=1, device_id=(dom, space), device_id_type=MESH)

    greet(k, prev_space, next_space)

    @pl.when(k > 0)
    def _():
        greet(k - 1, me, prev_space, next_space)

    @pl.when(k < doms - 1)
    def _():
        greet(k + 1, me, prev_space, next_space)

    def tile(q):
        return pl.ds(q * LANES, LANES)

    loads = []
    for q in range(tiles):
        loads.append(pltpu.make_async_copy(lev.at[:, tile(q)], lv.at[q], in_sem.at[0, q]))
        loads.append(pltpu.make_async_copy(obs.at[:, tile(q)], ov.at[q], in_sem.at[1, q]))
        loads.append(pltpu.make_async_copy(pert.at[:, :, tile(q)], pv.at[:, q], in_sem.at[2, q]))
        loads.append(pltpu.make_async_copy(ens.at[:, :, :, tile(q)], own.at[:, :, q, rows], in_sem.at[3, q]))
    for copy in loads:
        copy.start()

    def clear(ref, count):
        @pl.loop(0, count)
        def _(i):
            blank = jnp.zeros(ref.shape[1:-2] + (8, LANES), jnp.float32)
            ref[i, ..., TOP - 8 : TOP, :] = blank
            ref[i, ..., TOP + ny : TOP + ny + 8, :] = blank

    for ref in (own, ext, h0, s1, s2, b0):
        clear(ref, ref.shape[0])

    for copy in loads:
        copy.wait()

    gw[...], gd[0], gd[1], go[0], go[1] = level_of(lv[...].astype(jnp.float32), ov[...])

    def from_own(j):
        return jnp.clip(anc[k * pd + j] - k * pd, 0, pd - 1)

    def from_ext(j, low):
        parent = anc[k * pd + j]
        if low:
            return jnp.where(k == 0, j, jnp.clip(parent - (k * pd - CAP), 0, CAP - 1))
        return jnp.where(
            k == doms - 1, j - (pd - 2 * CAP), jnp.clip(parent - (k + 1) * pd, 0, CAP - 1) + CAP
        )

    @pl.loop(0, early // UNIT)
    def _(i):
        for s in range(UNIT):
            j = CAP + i * UNIT + s
            h0[j, :, rows] = 5.0 * (own[from_own(j), H_, :, rows] + pv[j])

    def column(ref, i, j, q):
        return jnp.concatenate(
            [ref[i, E_ : N_ + 1, q, rows], h0[j, q, rows][None], ref[i, C_:, q, rows]], axis=0
        )

    lane = lane_of((1, 1, LANES))
    half = lax.rem(lane, 64)

    def packed(ref, i, j, at, to_left, to_right):
        chosen = (lane >= at) & (lane < at + EDGE)
        to_left = jnp.where(chosen, pltpu.roll(column(ref, i, j, 0), at, 2), to_left)
        to_right = jnp.where(chosen, pltpu.roll(column(ref, i, j, tiles - 1), at + EDGE, 2), to_right)
        return to_left, to_right

    def message(rightward):
        return pltpu.make_async_remote_copy(
            src_ref=out1.at[int(rightward)],
            dst_ref=in1.at[int(rightward)],
            send_sem=msg_out_sem.at[int(rightward)],
            recv_sem=msg_in_sem.at[int(rightward)],
            device_id=(k, next_space if rightward else prev_space),
            device_id_type=MESH,
        )

    edge_to = (jnp.where(k < doms - 1, k + 1, k), jnp.where(k > 0, k - 1, k))
    edge_side = (jnp.where(k < doms - 1, 0, 1), jnp.where(k > 0, 1, 0))

    def edge_particle(up, t):
        if up:
            return jnp.where(k < doms - 1, pd - CAP + t, from_own(pd - CAP + t))
        return jnp.where(k > 0, t, from_own(t))

    def edge_message(up, rightward):
        at = 0 if up else 1
        return pltpu.make_async_remote_copy(
            src_ref=edge_out.at[at, int(rightward)],
            dst_ref=edge_in.at[edge_side[at], int(rightward)],
            send_sem=edge_out_sem.at[at, int(rightward)],
            recv_sem=edge_in_sem.at[edge_side[at], int(rightward)],
            device_id=(edge_to[at], next_space if rightward else prev_space),
            device_id_type=MESH,
        )

    def edge_arrival(side, rightward):
        return pltpu.make_async_remote_copy(
            src_ref=edge_out.at[side, int(rightward)],
            dst_ref=edge_in.at[side, int(rightward)],
            send_sem=edge_out_sem.at[side, int(rightward)],
            recv_sem=edge_in_sem.at[side, int(rightward)],
            device_id=(k, next_space if rightward else prev_space),
            device_id_type=MESH,
        )

    blank = jnp.zeros((4, ny, LANES), jnp.float32)
    for m, pairs in enumerate((8, (early - 16) // 2)):

        def pack(i, carry):
            for p in (2 * i, 2 * i + 1):
                for s in range(2):
                    j = CAP + 16 * m + 2 * p + s
                    carry = packed(own, from_own(j), j, 64 * s + 8 * p, *carry)
            return carry

        left, right = lax.fori_loop(0, pairs // 2, pack, (blank, blank))
        out1[0, 4 * m : 4 * m + 4] = left
        out1[1, 4 * m : 4 * m + 4] = right
    late = [pd - 2, pd - 1, 0, 1]
    levels = lv[...].astype(jnp.float32)
    for rightward in range(2):
        q, end = (tiles - 1, EDGE) if rightward else (0, 0)
        got = jnp.zeros((ny, LANES), jnp.float32)
        parts = [(levels[q], at) for at in (0, 64)] + [(ov[q], at) for at in (8, 72)]
        parts += [(5.0 * pv[j, q], 64 * (t % 2) + 16 + 8 * (t // 2)) for t, j in enumerate(late)]
        for part, at in parts:
            got = jnp.where((lane[0] >= at) & (lane[0] < at + EDGE), pltpu.roll(part, at + end, 1), got)
        out1[rightward, 8] = got
        for up in (True, False):
            for t in range(CAP):
                i = edge_particle(up, t)
                got = jnp.zeros((ny, LANES), jnp.float32)
                for f in range(4):
                    part = own[i, f, q, rows]
                    if f == H_:
                        part = 5.0 * part
                    at = 8 * f
                    got = jnp.where((lane[0] >= at) & (lane[0] < at + EDGE), pltpu.roll(part, at + end, 1), got)
                edge_out[0 if up else 1, rightward, t] = got + pltpu.roll(got, 64, 1)

    def unit(slots, src, where):
        for step in range(STEPS):
            last = step == STEPS - 1
            old, new = (None, s1) if step == 0 else (s1, s2) if step == 1 else (s2, s1)

            def reader(ref, s, y0):
                return lambda field, up: ref[s, field, :, pl.ds(TOP + y0 + up, HALF)]

            def first_reader(s, y0):
                return lambda field, up: (
                    h0[slots[s], :, pl.ds(TOP + y0 + up, HALF)]
                    if field == H_
                    else src[where[s], field, :, pl.ds(TOP + y0 + up, HALF)]
                )

            def read(s, y0):
                return first_reader(s, y0) if step == 0 else reader(old, s, y0)

            for s in range(UNIT):
                for y0 in range(0, ny, HALF):
                    e, n = flow(read(s, y0), gw[:, pl.ds(y0, HALF)], turn_of(ny, y0), True)
                    now = pl.ds(TOP + y0, HALF)
                    new[s, E_, :, now] = e
                    new[s, N_, :, now] = n
                    if last:
                        out[slots[s], E_, :, pl.ds(y0, HALF)] = e
                        out[slots[s], N_, :, pl.ds(y0, HALF)] = n
            for s in range(UNIT):
                for y0 in range(0, ny, HALF):
                    there = pl.ds(y0, HALF)
                    h, c = level(
                        read(s, y0), reader(new, s, y0), gd[int(last), :, there], go[int(last), :, there], last, True
                    )
                    if last:
                        out[slots[s], H_, :, there] = h
                        out[slots[s], C_, :, there] = c
                    else:
                        now = pl.ds(TOP + y0, HALF)
                        new[s, H_, :, now] = h
                        new[s, C_, :, now] = c

    def early_unit(i):
        slots = [CAP + i * UNIT + s for s in range(UNIT)]
        unit(slots, own, [from_own(j) for j in slots])

    pl.semaphore_wait(barrier, 2 + jnp.where(k > 0, 3, 0) + jnp.where(k < doms - 1, 3, 0))

    def dom_copy(up, q):
        first, lands, to = (pd - CAP, 0, k + 1) if up else (0, CAP, k - 1)
        return pltpu.make_async_remote_copy(
            src_ref=ens.at[first : first + CAP, :, :, tile(q)],
            dst_ref=ext.at[lands : lands + CAP, :, q, rows],
            send_sem=dom_out_sem.at[int(up), q],
            recv_sem=dom_in_sem.at[int(up), q],
            device_id=(to, me),
            device_id_type=MESH,
        )

    def send_particles(up, on):
        @pl.when(on)
        def _():
            for q in range(tiles):
                dom_copy(up, q).start()

    odd = lax.rem(k, 2) == 1
    send_particles(True, odd & (k < doms - 1))
    send_particles(False, jnp.logical_not(odd) & (k > 0))
    for rightward in (False, True):
        message(rightward).start()
        for up in (False, True):
            edge_message(up, rightward).start()
    send_particles(True, jnp.logical_not(odd))
    send_particles(False, odd)

    pl.loop(0, early // UNIT)(early_unit)

    @pl.when(k > 0)
    def _():
        for q in range(tiles):
            dom_copy(True, q).wait_recv()

    @pl.when(k < doms - 1)
    def _():
        for q in range(tiles):
            dom_copy(False, q).wait_recv()

    @pl.when(k == 0)
    def _():
        for s in range(CAP):
            ext[s, :, :, rows] = own[from_own(s), :, :, rows]

    @pl.when(k == doms - 1)
    def _():
        for s in range(CAP, 2 * CAP):
            ext[s, :, :, rows] = own[from_own(pd - 2 * CAP + s), :, :, rows]

    late_from = [from_ext(j, j < CAP) for j in late]
    for t, j in enumerate(late):
        h0[j, :, rows] = 5.0 * (ext[late_from[t], H_, :, rows] + pv[j])
    unit(late, ext, late_from)

    for rightward in (False, True):
        message(rightward).wait_recv()

    def ends(first, final, s, tile_so_far):
        base = 64 * s
        inner = (lane >= base + EDGE) & (lane < base + 3 * EDGE)
        tile_so_far = jnp.where(inner, pltpu.roll(first, base + EDGE, 2), tile_so_far)
        inner = (lane >= base + 32) & (lane < base + 32 + 2 * EDGE)
        return jnp.where(inner, pltpu.roll(final, (base + 32 + 2 * EDGE) % LANES, 2), tile_so_far)

    def beyond(from_left, from_right, at):
        shift_left = (LANES - at) % LANES if isinstance(at, int) else lax.rem(LANES - at, LANES)
        shift_right = (LANES + 44 - at) % LANES if isinstance(at, int) else lax.rem(LANES + 44 - at, LANES)
        got = jnp.where(half < EDGE, pltpu.roll(from_left, shift_left, 2), 0.0)
        return jnp.where((half >= 44) & (half < 44 + EDGE), pltpu.roll(from_right, shift_right, 2), got)

    fields = []
    for i, field in enumerate((levels, ov[...])):
        got = beyond(in1[1, 8:9], in1[0, 8:9], 8 * i)
        for s in range(2):
            got = ends(field[:1], field[tiles - 1 :], s, got)
        fields.append(got[0])
    gs[0], gs[1], gs[2], gs[3], gs[4] = level_of(*fields)

    def strip(c, p, got, ref, slots):
        for s, (i, j) in enumerate(slots):
            got = ends(column(ref, i, j, 0), column(ref, i, j, tiles - 1), s, got)
        b0[c, :, p, rows] = got

    def early_strip(c, p, m, p_in_message):
        got = beyond(in1[1, pl.ds(4 * m, 4)], in1[0, pl.ds(4 * m, 4)], 8 * p_in_message)
        first = CAP + 8 * c + 2 * p
        strip(c, p, got, own, [(from_own(first + s), first + s) for s in range(2)])

    whole = early // 8

    @pl.loop(0, whole)
    def _(c):
        for p in range(4):
            early_strip(c, p, c // 2, 4 * lax.rem(c, 2) + p)

    for p in range(2):
        early_strip(whole, p, 1, 4 * (whole - 2) + p)
    for side in range(2):
        for rightward in (False, True):
            edge_arrival(side, rightward).wait_recv()
    for p in range(2):
        side = 1 - p
        where = [late_from[2 * p + s] - CAP * side for s in range(2)]
        ways = [jnp.where(lane < 64, *(edge_in[side, w, where[s]][None] for s in range(2))) for w in range(2)]
        got = [beyond(ways[1], ways[0], 8 * f) for f in range(4)]
        got[H_] = got[H_] + beyond(in1[1, 8:9], in1[0, 8:9], 16 + 8 * p)
        slots = [(late_from[2 * p + s], late[2 * p + s]) for s in range(2)]
        strip(whole, 2 + p, jnp.concatenate(got, axis=0), ext, slots)

    for rightward in (False, True):
        message(rightward).wait_send()
        for up in (False, True):
            edge_message(up, rightward).wait_send()

    @pl.when(k < doms - 1)
    def _():
        for q in range(tiles):
            dom_copy(True, q).wait_send()

    @pl.when(k > 0)
    def _():
        for q in range(tiles):
            dom_copy(False, q).wait_send()


def finish(made, b0, gs, out, b1, b2, b3, sides, inner_sem, side_sem):
    pd, nf, tiles, ny, _ = made.shape
    lane = lane_of((1, 1, LANES))
    inner = [
        pltpu.make_async_copy(made.at[:, :, q], out.at[:, :, :, pl.ds(q * LANES, LANES)], inner_sem.at[q])
        for q in range(1, tiles - 1)
    ]
    for copy in inner:
        copy.start()

    for ref in (b1, b2, b3):
        blank = jnp.zeros(ref.shape[:-2] + (8, LANES), jnp.float32)
        ref[..., TOP - 8 : TOP, :] = blank
        ref[..., TOP + ny : TOP + ny + 8, :] = blank

    def leave(c, side, part):
        first, count = (CAP + 8 * c, 6) if part == 0 else (lax.rem(CAP + 8 * c + 6, pd), 2)
        at = side * (tiles - 1) * LANES
        return pltpu.make_async_copy(
            sides.at[side, pl.ds(first, count)],
            out.at[pl.ds(first, count), :, :, pl.ds(at, LANES)],
            side_sem.at[c, side, part],
        )

    def chunk(c):
        def reader(ref, y0):
            if ref is b0:
                return lambda field, up: ref[c, field, :, pl.ds(TOP + y0 + up, HALF)]
            return lambda field, up: ref[field, :, pl.ds(TOP + y0 + up, HALF)]

        for step in range(STEPS):
            last = step == STEPS - 1
            old, new = ((b0, b1), (b1, b2), (b2, b3))[step]
            for y0 in range(0, ny, HALF):
                now = pl.ds(TOP + y0, HALF)
                e, n = flow(reader(old, y0), gs[0, pl.ds(y0, HALF)][None], turn_of(ny, y0), False)
                new[E_, :, now] = e
                new[N_, :, now] = n
            depth, pull = (gs[2], gs[4]) if last else (gs[1], gs[3])
            for y0 in range(0, ny, HALF):
                now = pl.ds(TOP + y0, HALF)
                h, c_new = level(
                    reader(old, y0), reader(new, y0), depth[None, y0 : y0 + HALF], pull[None, y0 : y0 + HALF], last, False
                )
                new[H_, :, now] = h
                new[C_, :, now] = c_new
        for p in range(4):
            done = b3[:, p, TOP : TOP + ny]
            for s in range(2):
                base = 64 * s
                j = lax.rem(CAP + 8 * c + 2 * p + s, pd)
                at_left = pltpu.roll(done, LANES - EDGE - base, 2)
                at_right = pltpu.roll(done, (LANES - EDGE - (base + 32 + EDGE)) % LANES, 2)
                sides[0, j] = jnp.where(lane < EDGE, at_left, made[j, :, 0])
                sides[1, j] = jnp.where(lane >= LANES - EDGE, at_right, made[j, :, tiles - 1])
        for side in range(2):
            for part in range(2):
                leave(c, side, part).start()

    pl.loop(0, pd // 8)(chunk)

    for copy in inner:
        copy.wait()

    @pl.loop(0, pd // 8)
    def _(c):
        for side in range(2):
            for part in range(2):
                leave(c, side, part).wait()


def local(ensemble, ancestors, perturbation, levels, observed):
    pd, nf, ny, nx = ensemble.shape
    tiles = nx // LANES
    f32 = jnp.float32
    hbm = pl.BlockSpec(memory_space=pl.ANY)
    vmem = pl.BlockSpec(memory_space=pltpu.VMEM)
    made, strips, ground = pl.pallas_call(
        kernel,
        out_shape=[
            pltpu.VMEM((pd, nf, tiles, ny, LANES), f32),
            pltpu.VMEM((pd // 8, nf, 4, PITCH, LANES), f32),
            pltpu.VMEM((5, ny, LANES), f32),
        ],
        in_specs=[pl.BlockSpec(memory_space=pltpu.SMEM), hbm, hbm, hbm, hbm],
        out_specs=[vmem, vmem, vmem],
        scratch_shapes=[
            pltpu.VMEM((pd, nf, tiles, PITCH, LANES), f32),
            pltpu.VMEM((2 * CAP, nf, tiles, PITCH, LANES), f32),
            pltpu.VMEM((pd, tiles, PITCH, LANES), f32),
            pltpu.VMEM((pd, tiles, ny, LANES), f32),
            pltpu.VMEM((tiles, ny, LANES), jnp.int32),
            pltpu.VMEM((tiles, ny, LANES), f32),
            pltpu.VMEM((tiles, ny, LANES), f32),
            pltpu.VMEM((2, tiles, ny, LANES), f32),
            pltpu.VMEM((2, tiles, ny, LANES), f32),
            pltpu.VMEM((UNIT, nf, tiles, PITCH, LANES), f32),
            pltpu.VMEM((UNIT, nf, tiles, PITCH, LANES), f32),
            pltpu.VMEM((2, 9, ny, LANES), f32),
            pltpu.VMEM((2, 9, ny, LANES), f32),
            pltpu.VMEM((2, 2, CAP, ny, LANES), f32),
            pltpu.VMEM((2, 2, CAP, ny, LANES), f32),
            pltpu.SemaphoreType.DMA((4, tiles)),
            pltpu.SemaphoreType.DMA((2, tiles)),
            pltpu.SemaphoreType.DMA((2, tiles)),
            pltpu.SemaphoreType.DMA((2,)),
            pltpu.SemaphoreType.DMA((2,)),
            pltpu.SemaphoreType.DMA((2, 2)),
            pltpu.SemaphoreType.DMA((2, 2)),
        ],
        compiler_params=pltpu.CompilerParams(
            collective_id=0, has_side_effects=True, vmem_limit_bytes=40 * 1024 * 1024
        ),
        name="resample_and_step",
    )(*(pltpu.with_memory_space_constraint(x, pltpu.HBM) for x in (ancestors, ensemble, perturbation, levels, observed)))
    return pl.pallas_call(
        finish,
        out_shape=jax.ShapeDtypeStruct((pd, nf, ny, nx), f32),
        in_specs=[vmem, vmem, vmem],
        out_specs=hbm,
        scratch_shapes=[
            pltpu.VMEM((nf, 4, PITCH, LANES), f32),
            pltpu.VMEM((nf, 4, PITCH, LANES), f32),
            pltpu.VMEM((nf, 4, PITCH, LANES), f32),
            pltpu.VMEM((2, pd, nf, ny, LANES), f32),
            pltpu.SemaphoreType.DMA((tiles,)),
            pltpu.SemaphoreType.DMA((pd // 8, 2, 2)),
        ],
        compiler_params=pltpu.CompilerParams(vmem_limit_bytes=24 * 1024 * 1024),
        name="finish",
    )(made, strips, ground)


def solution(mesh):
    return jax.shard_map(
        local,
        mesh=mesh,
        in_specs=(
            P("dom", None, None, "space"),
            P(),
            P("dom", None, "space"),
            P(None, "space"),
            P(None, "space"),
        ),
        out_specs=P("dom", None, None, "space"),
        check_vma=False,
    )
```

time: 25.8 us -> 23.7 us (0.919)
  the two profiles are of different devices: /device:TPU:8 before, /device:TPU:7 now
where the time goes in v1:
time: 23.7 us; the launch traced here: 23.6 us
  Pallas kernels  23.6 us (100%)
    pallas_call x1, Pallas kernels, local(): pl.pallas_call(kernel, out_shape=[pltpu.VMEM((pd, nf, tiles, ny, LANES),...  20.2 us
    pallas_call x1, Pallas kernels, local(): pl.pallas_call(finish, out_shape=jax.ShapeDtypeStruct((pd, nf, ny, nx), f...  3.33 us

profile of v1, /device:TPU:7, one launch (start us, length us, event | category | flops | bytes accessed | tf_op | source)
XLA Modules:
  0.0 23.6 jit_solution(15790789331238118165)
XLA Ops:
  0.0 20.2 %resample_and_step.1 = (f32[32,4,4,16,128]{4,3,2,1,0:T(8,128)S(1)}, f32[4,4,4,32,128]{4,3,2,1,0:T(8,128)S(1)}, f32[5,16,128]{2,1,0:T(8,128)S(1)}) custom-call(s32[512]{0:T(512)} %anc.1, f32[32,4,16,512]{3,2,1,0:T(8,128)} %ens.1, f32[32,16,512]{2,1,0:T(8,128)} %pert.1, s32[16,512]{1,0:T(8,128)} %lev.1, f32[16,512]{1,0:T(8,128)} %obs.1), custom_call_target="tpu_custom_call" | custom-call | tf_op jit(solution)/shard_map/resample_and_step/pallas_call | solution.py:501
  20.2 3.3 %finish.1 = f32[32,4,16,512]{3,2,1,0:T(8,128)} custom-call(f32[32,4,4,16,128]{4,3,2,1,0:T(8,128)S(1)} %get-tuple-element.8.made, f32[4,4,4,32,128]{4,3,2,1,0:T(8,128)S(1)} %get-tuple-element.9.b0, f32[5,16,128]{2,1,0:T(8,128)S(1)} %get-tuple-element.10.gs), custom_call_target="tpu_custom_call" | custom-call | tf_op jit(solution)/shard_map/finish/pallas_call | solution.py:539

commit v2 on v1

v2 whole, which is shorter than its diff:
```python
import functools

import jax
import jax.numpy as jnp
from jax import lax
from jax.experimental import pallas as pl
from jax.experimental.pallas import tpu as pltpu
from jax.sharding import PartitionSpec as P

MESH = pl.DeviceIdType.MESH
STEPS = 3
CAP = 2
EDGE = 2 * STEPS
LANES = 128
TOP = 8
PITCH = 32
UNIT = 4
HALF = 8
PAIRS = 7
E_, N_, H_, C_ = range(4)


def lane_of(shape):
    return lax.broadcasted_iota(jnp.int32, shape, len(shape) - 1)


def east(cells, joined):
    turned = pltpu.roll(cells, LANES - 1, 2)
    if not joined:
        return turned
    following = jnp.concatenate([turned[1:], turned[:1]], axis=0)
    return jnp.where(lane_of(cells.shape) == LANES - 1, following, turned)


def west(cells, joined):
    turned = pltpu.roll(cells, 1, 2)
    if not joined:
        return turned
    preceding = jnp.concatenate([turned[-1:], turned[:-1]], axis=0)
    return jnp.where(lane_of(cells.shape) == 0, preceding, turned)


def flow(read, wet, turn, joined):
    e, n, h = read(E_, 0), read(N_, 0), read(H_, 0)
    e_new = wet * (
        (5.5 * e + turn * n)
        + (read(E_, 1) + read(E_, -1))
        + (east(e - h, joined) + west(e + h, joined))
    )
    n_new = wet * (
        (5.5 * n - turn * e)
        + (east(n, joined) + west(n, joined))
        + ((read(N_, 1) - read(H_, 1)) + (read(N_, -1) + read(H_, -1)))
    )
    return e_new, n_new


def level(read, read_new, depth, pull, last, joined):
    e, n = read_new(E_, 0), read_new(N_, 0)
    spread = (east(e, joined) - west(e, joined)) + (read_new(N_, 1) - read_new(N_, -1))
    h_new = ((0.18 if last else 0.9) * read(H_, 0) + pull) - depth * spread
    c = read(C_, 0)
    c_east, c_west = east(c, joined), west(c, joined)
    c_north, c_south = read(C_, 1), read(C_, -1)
    c_new = (
        (6.0 * c + ((c_east + c_west) + (c_north + c_south)))
        - e * (c_east - c_west)
        - n * (c_north - c_south)
    )
    if last:
        c_new = 0.001 * c_new
    return h_new, c_new


def level_of(levels, observed):
    return (
        jnp.where(levels > 0, 0.1, 0.0).astype(jnp.float32),
        1.25 * levels,
        0.25 * levels,
        0.5 * observed,
        0.1 * observed,
    )


def turn_of(ny, y0):
    y = lax.broadcasted_iota(jnp.int32, (1, HALF, LANES), 1).astype(jnp.float32) + float(y0)
    return 2.0 * (0.2 + 0.6 * y / ny)


def all_steps(first, s1, s2, ground, keep, joined, ny, parts):
    wet, depth, pull = ground
    count = len(parts)
    for step in range(STEPS):
        last = step == STEPS - 1
        old, new = (None, s1) if step == 0 else (s1, s2) if step == 1 else (s2, s1)

        def reader(ref, i, y0):
            return lambda field, up: parts[i](ref, field, pl.ds(TOP + y0 + up, HALF))[...]

        def read(i, y0):
            return (lambda field, up: first(i, field, y0, up)) if step == 0 else reader(old, i, y0)

        for i in range(count):
            for y0 in range(0, ny, HALF):
                e, n = flow(read(i, y0), wet(y0), turn_of(ny, y0), joined)
                now = pl.ds(TOP + y0, HALF)
                parts[i](new, E_, now)[...] = e
                parts[i](new, N_, now)[...] = n
                if last:
                    keep(i, E_, y0, e)
                    keep(i, N_, y0, n)
        for i in range(count):
            for y0 in range(0, ny, HALF):
                h, c = level(read(i, y0), reader(new, i, y0), depth(last, y0), pull(last, y0), last, joined)
                now = pl.ds(TOP + y0, HALF)
                if last:
                    keep(i, H_, y0, h)
                    keep(i, C_, y0, c)
                else:
                    parts[i](new, H_, now)[...] = h
                    parts[i](new, C_, now)[...] = c


def slot_parts():
    return [lambda ref, field, now, s=s: ref.at[s, field, :, now] for s in range(UNIT)]


def row_ground(gw, gd, go):
    return (
        lambda y0: gw[:, pl.ds(y0, HALF)],
        lambda last, y0: gd[int(last), :, pl.ds(y0, HALF)],
        lambda last, y0: go[int(last), :, pl.ds(y0, HALF)],
    )


def strip_ground(gs):
    return (
        lambda y0: gs[0, pl.ds(y0, HALF)][None],
        lambda last, y0: gs[2 if last else 1, pl.ds(y0, HALF)][None],
        lambda last, y0: gs[4 if last else 3, pl.ds(y0, HALF)][None],
    )


def step_strips(b0, b1, b2, b3, gs, groups, ny):
    parts = [lambda ref, field, now, g=g: ref.at[field, g, now] for g in groups]

    def keep(i, field, y0, value):
        b3[field, groups[i], pl.ds(y0, HALF)] = value

    all_steps(
        lambda i, field, y0, up: b0[field, groups[i], pl.ds(TOP + y0 + up, HALF)],
        b1, b2, strip_ground(gs), keep, False, ny, parts,
    )


def put_strips(b3, p, slots, out):
    done = b3[:, p]
    lane = lane_of(done.shape)
    final = out.shape[2] - 1
    for s, j in enumerate(slots):
        base = 64 * s
        at_left = pltpu.roll(done, LANES - EDGE - base, 2)
        at_right = pltpu.roll(done, (LANES - EDGE - (base + 32 + EDGE)) % LANES, 2)
        pltpu.store(out.at[j, :, 0], at_left, mask=lane < EDGE)
        pltpu.store(out.at[j, :, final], at_right, mask=lane >= LANES - EDGE)


def clear_rows(ref, ny):
    @pl.loop(0, ref.shape[0])
    def _(i):
        blank = jnp.zeros(ref.shape[1:-2] + (8, LANES), jnp.float32)
        ref[i, ..., TOP - 8 : TOP, :] = blank
        ref[i, ..., TOP + ny : TOP + ny + 8, :] = blank


def kernel(
    anc_in, ens, pert, lev, obs, out, late0, late_strips, gs, gw, gd, go,
    anc, ends_of, inner, ext, h0, pv, lv, ov, s1, s2, b0, b1, b2, b3, out1, in1, edge_out, edge_in,
    in_sem, dom_out_sem, dom_in_sem, msg_out_sem, msg_in_sem, edge_out_sem, edge_in_sem,
):
    pd = ens.shape[0]
    ny = ens.shape[2]
    tiles = ens.shape[3] // LANES
    doms, spaces = lax.axis_size("dom"), lax.axis_size("space")
    k, me = lax.axis_index("dom"), lax.axis_index("space")
    prev_space, next_space = lax.rem(me + spaces - 1, spaces), lax.rem(me + 1, spaces)
    early = pd - 2 * CAP
    rows = slice(TOP, TOP + ny)

    barrier = pltpu.get_barrier_semaphore()

    def greet(dom, *spaces_there):
        for space in spaces_there:
            pl.semaphore_signal(barrier, inc=1, device_id=(dom, space), device_id_type=MESH)

    greet(k, prev_space, next_space)

    @pl.when(k > 0)
    def _():
        greet(k - 1, me, prev_space, next_space)

    @pl.when(k < doms - 1)
    def _():
        greet(k + 1, me, prev_space, next_space)

    def tile(q):
        return pl.ds(q * LANES, LANES)

    needed_first, needed_next = [pltpu.make_async_copy(anc_in, anc, in_sem.at[4, 0])], []
    for q in (0, tiles - 1, *range(1, tiles - 1)):
        at_end = q in (0, tiles - 1)
        loads = needed_first if at_end else needed_next
        here = ends_of.at[:, :, int(q > 0), rows] if at_end else inner.at[:, :, q - 1, rows]
        loads.append(pltpu.make_async_copy(ens.at[:, :, :, tile(q)], here, in_sem.at[3, q]))
        loads.append(pltpu.make_async_copy(pert.at[:, :, tile(q)], pv.at[:, q], in_sem.at[2, q]))
        loads.append(pltpu.make_async_copy(lev.at[:, tile(q)], lv.at[q], in_sem.at[0, q]))
        loads.append(pltpu.make_async_copy(obs.at[:, tile(q)], ov.at[q], in_sem.at[1, q]))
    for copy in needed_first + needed_next:
        copy.start()

    for ref in (ends_of, inner, h0, late0, s1, s2, b0, b1, b2, late_strips):
        clear_rows(ref, ny)

    for copy in needed_first:
        copy.wait()

    def from_own(j):
        return jnp.clip(anc[k * pd + j] - k * pd, 0, pd - 1)

    def from_ext(j, low):
        parent = anc[k * pd + j]
        if low:
            return jnp.where(k == 0, j, jnp.clip(parent - (k * pd - CAP), 0, CAP - 1))
        return jnp.where(
            k == doms - 1, j - (pd - 2 * CAP), jnp.clip(parent - (k + 1) * pd, 0, CAP - 1) + CAP
        )

    def column(i, j, side):
        h = 5.0 * (ends_of[i, H_, side, rows] + pv[j, side * (tiles - 1)])
        return jnp.concatenate(
            [ends_of[i, E_ : N_ + 1, side, rows], h[None], ends_of[i, C_:, side, rows]], axis=0
        )

    full = lane_of((4, ny, LANES))
    flat = lane_of((ny, LANES))

    def message(rightward):
        return pltpu.make_async_remote_copy(
            src_ref=out1.at[int(rightward)],
            dst_ref=in1.at[int(rightward)],
            send_sem=msg_out_sem.at[int(rightward)],
            recv_sem=msg_in_sem.at[int(rightward)],
            device_id=(k, next_space if rightward else prev_space),
            device_id_type=MESH,
        )

    edge_to = (jnp.where(k < doms - 1, k + 1, k), jnp.where(k > 0, k - 1, k))
    edge_side = (jnp.where(k < doms - 1, 0, 1), jnp.where(k > 0, 1, 0))

    def edge_particle(up, t):
        if up:
            return jnp.where(k < doms - 1, pd - CAP + t, from_own(pd - CAP + t))
        return jnp.where(k > 0, t, from_own(t))

    def edge_message(up, rightward):
        at = 0 if up else 1
        return pltpu.make_async_remote_copy(
            src_ref=edge_out.at[at, int(rightward)],
            dst_ref=edge_in.at[edge_side[at], int(rightward)],
            send_sem=edge_out_sem.at[at, int(rightward)],
            recv_sem=edge_in_sem.at[edge_side[at], int(rightward)],
            device_id=(edge_to[at], next_space if rightward else prev_space),
            device_id_type=MESH,
        )

    def edge_arrival(side, rightward):
        return pltpu.make_async_remote_copy(
            src_ref=edge_out.at[side, int(rightward)],
            dst_ref=edge_in.at[side, int(rightward)],
            send_sem=edge_out_sem.at[side, int(rightward)],
            recv_sem=edge_in_sem.at[side, int(rightward)],
            device_id=(k, next_space if rightward else prev_space),
            device_id_type=MESH,
        )

    @pl.loop(0, early // (2 * PAIRS))
    def _(m):
        to_left = jnp.zeros((4, ny, LANES), jnp.float32)
        to_right = to_left
        for p in range(PAIRS):
            for s in range(2):
                at = 64 * s + 8 * p
                j = CAP + 2 * (PAIRS * m + p) + s
                i = from_own(j)
                chosen = (full >= at) & (full < at + EDGE)
                to_left = jnp.where(chosen, pltpu.roll(column(i, j, 0), at, 2), to_left)
                to_right = jnp.where(chosen, pltpu.roll(column(i, j, 1), at + EDGE, 2), to_right)
        out1[0, pl.ds(4 * m, 4)] = to_left
        out1[1, pl.ds(4 * m, 4)] = to_right

    late = [pd - 2, pd - 1, 0, 1]
    for rightward in range(2):
        q, end = (tiles - 1, EDGE) if rightward else (0, 0)
        got = jnp.zeros((ny, LANES), jnp.float32)
        parts = [(lv[q].astype(jnp.float32), at) for at in (0, 64)] + [(ov[q], at) for at in (8, 72)]
        parts += [(5.0 * pv[j, q], 64 * (t % 2) + 16 + 8 * (t // 2)) for t, j in enumerate(late)]
        for part, at in parts:
            got = jnp.where((flat >= at) & (flat < at + EDGE), pltpu.roll(part, at + end, 1), got)
        out1[rightward, 8] = got
        for up in (True, False):
            for t in range(CAP):
                i = edge_particle(up, t)
                got = jnp.zeros((ny, LANES), jnp.float32)
                for f in range(4):
                    part = ends_of[i, f, rightward, rows]
                    if f == H_:
                        part = 5.0 * part
                    at = 8 * f
                    got = jnp.where((flat >= at) & (flat < at + EDGE), pltpu.roll(part, at + end, 1), got)
                edge_out[0 if up else 1, rightward, t] = got + pltpu.roll(got, 64, 1)

    pl.semaphore_wait(barrier, 2 + jnp.where(k > 0, 3, 0) + jnp.where(k < doms - 1, 3, 0))

    def dom_copy(up, q):
        first, lands, to = (pd - CAP, 0, k + 1) if up else (0, CAP, k - 1)
        return pltpu.make_async_remote_copy(
            src_ref=ens.at[first : first + CAP, :, :, tile(q)],
            dst_ref=ext.at[lands : lands + CAP, :, q],
            send_sem=dom_out_sem.at[int(up), q],
            recv_sem=dom_in_sem.at[int(up), q],
            device_id=(to, me),
            device_id_type=MESH,
        )

    def send_particles(up, on):
        @pl.when(on)
        def _():
            for q in range(tiles):
                dom_copy(up, q).start()

    for rightward in (True, False):
        message(rightward).start()
        for up in (False, True):
            edge_message(up, rightward).start()
    odd = lax.rem(k, 2) == 1
    send_particles(True, odd & (k < doms - 1))
    send_particles(False, jnp.logical_not(odd) & (k > 0))
    send_particles(True, jnp.logical_not(odd))
    send_particles(False, odd)

    for copy in needed_next:
        copy.wait()

    levels = lv[...].astype(jnp.float32)
    gw[...], gd[0], gd[1], go[0], go[1] = level_of(levels, ov[...])

    def whole_rows(i, f, at):
        return jnp.concatenate([ends_of[i, f, :1, at], inner[i, f, :, at], ends_of[i, f, 1:, at]], axis=0)

    @pl.loop(0, early // UNIT)
    def _(u):
        for s in range(UNIT):
            j = CAP + u * UNIT + s
            h0[j, :, rows] = 5.0 * (whole_rows(from_own(j), H_, rows) + pv[j])

    @pl.loop(0, early // UNIT)
    def _(u):
        slots = [CAP + u * UNIT + s for s in range(UNIT)]
        where = [from_own(j) for j in slots]

        def first(i, field, y0, up):
            at = pl.ds(TOP + y0 + up, HALF)
            return h0[slots[i], :, at] if field == H_ else whole_rows(where[i], field, at)

        def keep(i, field, y0, value):
            out[slots[i], field, :, pl.ds(y0, HALF)] = value

        all_steps(first, s1, s2, row_ground(gw, gd, go), keep, True, ny, slot_parts())

    for rightward in (False, True):
        message(rightward).wait_recv()

    def ends(first, final, s, tile_so_far):
        base = 64 * s
        lane = lane_of(first.shape)
        chosen = (lane >= base + EDGE) & (lane < base + 3 * EDGE)
        tile_so_far = jnp.where(chosen, pltpu.roll(first, base + EDGE, 2), tile_so_far)
        chosen = (lane >= base + 32) & (lane < base + 32 + 2 * EDGE)
        return jnp.where(chosen, pltpu.roll(final, (base + 32 + 2 * EDGE) % LANES, 2), tile_so_far)

    def beyond(from_left, from_right, at):
        half = lax.rem(lane_of(from_left.shape), 64)
        got = jnp.where(half < EDGE, pltpu.roll(from_left, (LANES - at) % LANES, 2), 0.0)
        chosen = (half >= 44) & (half < 44 + EDGE)
        return jnp.where(chosen, pltpu.roll(from_right, (LANES + 44 - at) % LANES, 2), got)

    fields = []
    for i, field in enumerate((levels, ov[...])):
        got = beyond(in1[1, 8:9], in1[0, 8:9], 8 * i)
        for s in range(2):
            got = ends(field[:1], field[tiles - 1 :], s, got)
        fields.append(got[0])
    gs[0], gs[1], gs[2], gs[3], gs[4] = level_of(*fields)

    @pl.loop(0, early // (2 * PAIRS))
    def _(m):
        from_left, from_right = in1[1, pl.ds(4 * m, 4)], in1[0, pl.ds(4 * m, 4)]
        slots = [[CAP + 2 * (PAIRS * m + p) + s for s in range(2)] for p in range(PAIRS)]
        for p in range(PAIRS):
            got = beyond(from_left, from_right, 8 * p)
            for s, j in enumerate(slots[p]):
                i = from_own(j)
                got = ends(column(i, j, 0), column(i, j, 1), s, got)
            b0[:, p, rows] = got
        step_strips(b0, b1, b2, b3, gs, [slice(0, 4), slice(4, PAIRS)], ny)
        for p in range(PAIRS):
            put_strips(b3, p, slots[p], out)

    @pl.when(k > 0)
    def _():
        for q in range(tiles):
            dom_copy(True, q).wait_recv()

    @pl.when(k < doms - 1)
    def _():
        for q in range(tiles):
            dom_copy(False, q).wait_recv()

    def own_particle(lands, j):
        for f in range(4):
            ext[lands, f] = whole_rows(from_own(j), f, rows)

    @pl.when(k == 0)
    def _():
        for s in range(CAP):
            own_particle(s, s)

    @pl.when(k == doms - 1)
    def _():
        for s in range(CAP, 2 * CAP):
            own_particle(s, pd - 2 * CAP + s)

    late_from = [from_ext(j, j < CAP) for j in late]
    for t, j in enumerate(late):
        for f in range(4):
            state = ext[late_from[t], f]
            late0[t, f, :, rows] = 5.0 * (state + pv[j]) if f == H_ else state

    for side in range(2):
        for rightward in (False, True):
            edge_arrival(side, rightward).wait_recv()
    for p in range(2):
        side = 1 - p
        where = [late_from[2 * p + s] - CAP * side for s in range(2)]
        ways = [jnp.where(flat < 64, *(edge_in[side, w, where[s]] for s in range(2)))[None] for w in range(2)]
        got = [beyond(ways[1], ways[0], 8 * f) for f in range(4)]
        got[H_] = got[H_] + beyond(in1[1, 8:9], in1[0, 8:9], 16 + 8 * p)
        got = jnp.concatenate(got, axis=0)
        for s in range(2):
            got = ends(late0[2 * p + s, :, 0, rows], late0[2 * p + s, :, tiles - 1, rows], s, got)
        late_strips[:, p, rows] = got

    for rightward in (False, True):
        message(rightward).wait_send()
        for up in (False, True):
            edge_message(up, rightward).wait_send()

    @pl.when(k < doms - 1)
    def _():
        for q in range(tiles):
            dom_copy(True, q).wait_send()

    @pl.when(k > 0)
    def _():
        for q in range(tiles):
            dom_copy(False, q).wait_send()


def finish(made, late0, late_strips, gs, gw, gd, go, out, late_out, s1, s2, b1, b2, b3, sem):
    pd, nf, tiles, ny, _ = made.shape

    def tile(q):
        return pl.ds(q * LANES, LANES)

    copies = [
        pltpu.make_async_copy(made.at[CAP : pd - CAP, :, q], out.at[CAP : pd - CAP, :, :, tile(q)], sem.at[0, q])
        for q in range(tiles)
    ]
    for copy in copies:
        copy.start()
    for ref in (s1, s2, b1, b2):
        clear_rows(ref, ny)

    def keep(i, field, y0, value):
        late_out[i, field, :, pl.ds(y0, HALF)] = value

    all_steps(
        lambda i, field, y0, up: late0[i, field, :, pl.ds(TOP + y0 + up, HALF)],
        s1, s2, row_ground(gw, gd, go), keep, True, ny, slot_parts(),
    )
    step_strips(late_strips, b1, b2, b3, gs, [slice(0, CAP)], ny)
    for p in range(2):
        put_strips(b3, p, [2 * p, 2 * p + 1], late_out)
    for p, first in enumerate((pd - CAP, 0)):
        for q in range(tiles):
            copy = pltpu.make_async_copy(
                late_out.at[CAP * p : CAP * p + CAP, :, q], out.at[first : first + CAP, :, :, tile(q)], sem.at[1 + p, q]
            )
            copy.start()
            copies.append(copy)
    for copy in copies:
        copy.wait()


def local(ensemble, ancestors, perturbation, levels, observed):
    pd, nf, ny, nx = ensemble.shape
    tiles = nx // LANES
    f32 = jnp.float32
    hbm = pl.BlockSpec(memory_space=pl.ANY)
    vmem = pl.BlockSpec(memory_space=pltpu.VMEM)
    state = (UNIT, nf, tiles, PITCH, LANES)
    handed = [
        pltpu.VMEM((pd, nf, tiles, ny, LANES), f32),
        pltpu.VMEM(state, f32),
        pltpu.VMEM((nf, CAP, PITCH, LANES), f32),
        pltpu.VMEM((5, ny, LANES), f32),
        pltpu.VMEM((tiles, ny, LANES), f32),
        pltpu.VMEM((2, tiles, ny, LANES), f32),
        pltpu.VMEM((2, tiles, ny, LANES), f32),
    ]
    between = pl.pallas_call(
        kernel,
        out_shape=handed,
        in_specs=[hbm] * 5,
        out_specs=[vmem] * len(handed),
        scratch_shapes=[
            pltpu.SMEM(ancestors.shape, jnp.int32),
            pltpu.VMEM((pd, nf, 2, PITCH, LANES), f32),
            pltpu.VMEM((pd, nf, tiles - 2, PITCH, LANES), f32),
            pltpu.VMEM((2 * CAP, nf, tiles, ny, LANES), f32),
            pltpu.VMEM((pd, tiles, PITCH, LANES), f32),
            pltpu.VMEM((pd, tiles, ny, LANES), f32),
            pltpu.VMEM((tiles, ny, LANES), jnp.int32),
            pltpu.VMEM((tiles, ny, LANES), f32),
            pltpu.VMEM(state, f32),
            pltpu.VMEM(state, f32),
            pltpu.VMEM((nf, PAIRS, PITCH, LANES), f32),
            pltpu.VMEM((nf, PAIRS, PITCH, LANES), f32),
            pltpu.VMEM((nf, PAIRS, PITCH, LANES), f32),
            pltpu.VMEM((nf, PAIRS, ny, LANES), f32),
            pltpu.VMEM((2, 9, ny, LANES), f32),
            pltpu.VMEM((2, 9, ny, LANES), f32),
            pltpu.VMEM((2, 2, CAP, ny, LANES), f32),
            pltpu.VMEM((2, 2, CAP, ny, LANES), f32),
            pltpu.SemaphoreType.DMA((5, tiles)),
            pltpu.SemaphoreType.DMA((2, tiles)),
            pltpu.SemaphoreType.DMA((2, tiles)),
            pltpu.SemaphoreType.DMA((2,)),
            pltpu.SemaphoreType.DMA((2,)),
            pltpu.SemaphoreType.DMA((2, 2)),
            pltpu.SemaphoreType.DMA((2, 2)),
        ],
        compiler_params=pltpu.CompilerParams(
            collective_id=0, has_side_effects=True, vmem_limit_bytes=40 * 1024 * 1024
        ),
        name="resample_and_step",
    )(*(pltpu.with_memory_space_constraint(x, pltpu.HBM) for x in (ancestors, ensemble, perturbation, levels, observed)))
    return pl.pallas_call(
        finish,
        out_shape=jax.ShapeDtypeStruct((pd, nf, ny, nx), f32),
        in_specs=[vmem] * len(handed),
        out_specs=hbm,
        scratch_shapes=[
            pltpu.VMEM((UNIT, nf, tiles, ny, LANES), f32),
            pltpu.VMEM(state, f32),
            pltpu.VMEM(state, f32),
            pltpu.VMEM((nf, CAP, PITCH, LANES), f32),
            pltpu.VMEM((nf, CAP, PITCH, LANES), f32),
            pltpu.VMEM((nf, CAP, ny, LANES), f32),
            pltpu.SemaphoreType.DMA((3, tiles)),
        ],
        compiler_params=pltpu.CompilerParams(vmem_limit_bytes=24 * 1024 * 1024),
        name="finish",
    )(*between)


def solution(mesh):
    return jax.shard_map(
        local,
        mesh=mesh,
        in_specs=(
            P("dom", None, None, "space"),
            P(),
            P("dom", None, "space"),
            P(None, "space"),
            P(None, "space"),
        ),
        out_specs=P("dom", None, None, "space"),
        check_vma=False,
    )
```

time: 23.7 us -> 21.2 us (0.89)
  the two profiles are of different devices: /device:TPU:7 before, /device:TPU:1 now
where the time goes in v2:
time: 21.2 us; the launch traced here: 21.1 us
  Pallas kernels  21.1 us (100%)
    pallas_call x1, Pallas kernels, local(): pl.pallas_call(kernel, out_shape=handed, in_specs=[hbm] * 5, out_specs=[v...  18.7 us
    pallas_call x1, Pallas kernels, local(): pl.pallas_call(finish, out_shape=jax.ShapeDtypeStruct((pd, nf, ny, nx), f...  2.37 us

profile of v2, /device:TPU:1, one launch (start us, length us, event | category | flops | bytes accessed | tf_op | source)
XLA Modules:
  0.0 21.1 jit_solution(4466322937657620686)
XLA Ops:
  0.0 18.7 %resample_and_step.1 = (f32[32,4,4,16,128]{4,3,2,1,0:T(8,128)S(1)}, f32[4,4,4,32,128]{4,3,2,1,0:T(8,128)S(1)}, f32[4,2,32,128]{3,2,1,0:T(8,128)S(1)}, f32[5,16,1...) custom-call(s32[512]{0:T(512)} %anc_in.1, ...), custom_call_target="tpu_custom_call" | custom-call | tf_op jit(solution)/shard_map/resample_and_step/pallas_call | solution.py:531
  18.7 2.4 %finish.1 = f32[32,4,16,512]{3,2,1,0:T(8,128)} custom-call(f32[32,4,4,16,128]{4,3,2,1,0:T(8,128)S(1)} %get-tuple-element.12.made, f32[4,4,4,32,128]{4,3,2,1,0:T(8,128)S(1)} %get-tuple-element.13.late0, f32[4,2,32,128]{3,2,1,0:T(8,128)S(1)} %get-tuple-element.14.late_strips, f32[5,16,128]{2,1,0:T(8,128)S(1)} %get-tuple-element.15.gs, ...), custom_call_target="tpu_custom_call" | custom-call | tf_op jit(solution)/shard_map/finish/pallas_call | solution.py:568

commit v3 on v2

--- a/solution.py
+++ b/solution.py
@@ -17,6 +17,12 @@
 UNIT = 4
 HALF = 8
 PAIRS = 7
+RUN = 8
+AHEAD = 4
+NEED = (EDGE, EDGE - 1, EDGE, EDGE - 3)
+SHELF = (0, 12, 6, 17)
+SLOT_LANES = 20
+TRIPLE = 3
 E_, N_, H_, C_ = range(4)
 
 
@@ -241,7 +247,6 @@
             [ends_of[i, E_ : N_ + 1, side, rows], h[None], ends_of[i, C_:, side, rows]], axis=0
         )
 
-    full = lane_of((4, ny, LANES))
     flat = lane_of((ny, LANES))
 
     def message(rightward):
@@ -283,21 +288,31 @@
             device_id_type=MESH,
         )
 
+    def shelve(columns, side, at, tile_so_far):
+        for f in range(4):
+            first = LANES - NEED[f] if side else 0
+            to = at + SHELF[f]
+            chosen = (flat >= to) & (flat < to + NEED[f])
+            tile_so_far = jnp.where(chosen, pltpu.roll(columns[f], (to - first) % LANES, 1), tile_so_far)
+        return tile_so_far
+
+    shelves = -(-PAIRS // TRIPLE)
+
     @pl.loop(0, early // (2 * PAIRS))
     def _(m):
-        to_left = jnp.zeros((4, ny, LANES), jnp.float32)
-        to_right = to_left
-        for p in range(PAIRS):
-            for s in range(2):
-                at = 64 * s + 8 * p
-                j = CAP + 2 * (PAIRS * m + p) + s
-                i = from_own(j)
-                chosen = (full >= at) & (full < at + EDGE)
-                to_left = jnp.where(chosen, pltpu.roll(column(i, j, 0), at, 2), to_left)
-                to_right = jnp.where(chosen, pltpu.roll(column(i, j, 1), at + EDGE, 2), to_right)
-        out1[0, pl.ds(4 * m, 4)] = to_left
-        out1[1, pl.ds(4 * m, 4)] = to_right
-
+        for r in range(shelves):
+            packed = [jnp.zeros((ny, LANES), jnp.float32)] * 2
+            for p in range(TRIPLE * r, min(PAIRS, TRIPLE * r + TRIPLE)):
+                for s in range(2):
+                    j = CAP + 2 * (PAIRS * m + p) + s
+                    i = from_own(j)
+                    for side in range(2):
+                        at = 64 * s + SLOT_LANES * (p - TRIPLE * r)
+                        packed[side] = shelve(column(i, j, side), side, at, packed[side])
+            for side in range(2):
+                out1[side, shelves * m + r] = packed[side]
+
+    extra = shelves * (early // (2 * PAIRS))
     late = [pd - 2, pd - 1, 0, 1]
     for rightward in range(2):
         q, end = (tiles - 1, EDGE) if rightward else (0, 0)
@@ -306,20 +321,15 @@
         parts += [(5.0 * pv[j, q], 64 * (t % 2) + 16 + 8 * (t // 2)) for t, j in enumerate(late)]
         for part, at in parts:
             got = jnp.where((flat >= at) & (flat < at + EDGE), pltpu.roll(part, at + end, 1), got)
-        out1[rightward, 8] = got
+        out1[rightward, extra] = got
         for up in (True, False):
+            got = jnp.zeros((ny, LANES), jnp.float32)
             for t in range(CAP):
                 i = edge_particle(up, t)
-                got = jnp.zeros((ny, LANES), jnp.float32)
-                for f in range(4):
-                    part = ends_of[i, f, rightward, rows]
-                    if f == H_:
-                        part = 5.0 * part
-                    at = 8 * f
-                    got = jnp.where((flat >= at) & (flat < at + EDGE), pltpu.roll(part, at + end, 1), got)
-                edge_out[0 if up else 1, rightward, t] = got + pltpu.roll(got, 64, 1)
-
-    pl.semaphore_wait(barrier, 2 + jnp.where(k > 0, 3, 0) + jnp.where(k < doms - 1, 3, 0))
+                columns = [ends_of[i, f, rightward, rows] for f in range(4)]
+                columns[H_] = 5.0 * columns[H_]
+                got = shelve(columns, rightward, 64 * t, got)
+            edge_out[0 if up else 1, rightward] = got
 
     def dom_copy(up, q):
         first, lands, to = (pd - CAP, 0, k + 1) if up else (0, CAP, k - 1)
@@ -338,15 +348,21 @@
             for q in range(tiles):
                 dom_copy(up, q).start()
 
-    for rightward in (True, False):
-        message(rightward).start()
-        for up in (False, True):
-            edge_message(up, rightward).start()
     odd = lax.rem(k, 2) == 1
-    send_particles(True, odd & (k < doms - 1))
-    send_particles(False, jnp.logical_not(odd) & (k > 0))
-    send_particles(True, jnp.logical_not(odd))
-    send_particles(False, odd)
+
+    def send():
+        pl.semaphore_wait(barrier, 2 + jnp.where(k > 0, 3, 0) + jnp.where(k < doms - 1, 3, 0))
+        for rightward in (True, False):
+            message(rightward).start()
+            for up in (False, True):
+                edge_message(up, rightward).start()
+        send_particles(True, odd & (k < doms - 1))
+        send_particles(False, jnp.logical_not(odd) & (k > 0))
+        send_particles(True, jnp.logical_not(odd))
+        send_particles(False, odd)
+
+    ahead = lax.rem(me, RUN) == 0
+    pl.when(jnp.logical_not(ahead))(send)
 
     for copy in needed_next:
         copy.wait()
@@ -365,6 +381,7 @@
 
     @pl.loop(0, early // UNIT)
     def _(u):
+        pl.when(ahead & (u == AHEAD))(send)
         slots = [CAP + u * UNIT + s for s in range(UNIT)]
         where = [from_own(j) for j in slots]
 
@@ -388,15 +405,19 @@
         chosen = (lane >= base + 32) & (lane < base + 32 + 2 * EDGE)
         return jnp.where(chosen, pltpu.roll(final, (base + 32 + 2 * EDGE) % LANES, 2), tile_so_far)
 
-    def beyond(from_left, from_right, at):
+    def beyond(from_left, from_right, at, width=EDGE):
         half = lax.rem(lane_of(from_left.shape), 64)
-        got = jnp.where(half < EDGE, pltpu.roll(from_left, (LANES - at) % LANES, 2), 0.0)
-        chosen = (half >= 44) & (half < 44 + EDGE)
-        return jnp.where(chosen, pltpu.roll(from_right, (LANES + 44 - at) % LANES, 2), got)
+        chosen = (half >= EDGE - width) & (half < EDGE)
+        got = jnp.where(chosen, pltpu.roll(from_left, (LANES + EDGE - width - at) % LANES, 1), 0.0)
+        chosen = (half >= 44) & (half < 44 + width)
+        return jnp.where(chosen, pltpu.roll(from_right, (LANES + 44 - at) % LANES, 1), got)
+
+    def unshelved(from_left, from_right, at):
+        return [beyond(from_left, from_right, at + SHELF[f], NEED[f]) for f in range(4)]
 
     fields = []
     for i, field in enumerate((levels, ov[...])):
-        got = beyond(in1[1, 8:9], in1[0, 8:9], 8 * i)
+        got = beyond(in1[1, extra], in1[0, extra], 8 * i)[None]
         for s in range(2):
             got = ends(field[:1], field[tiles - 1 :], s, got)
         fields.append(got[0])
@@ -404,10 +425,10 @@
 
     @pl.loop(0, early // (2 * PAIRS))
     def _(m):
-        from_left, from_right = in1[1, pl.ds(4 * m, 4)], in1[0, pl.ds(4 * m, 4)]
         slots = [[CAP + 2 * (PAIRS * m + p) + s for s in range(2)] for p in range(PAIRS)]
         for p in range(PAIRS):
-            got = beyond(from_left, from_right, 8 * p)
+            r = shelves * m + p // TRIPLE
+            got = jnp.stack(unshelved(in1[1, r], in1[0, r], SLOT_LANES * (p % TRIPLE)))
             for s, j in enumerate(slots[p]):
                 i = from_own(j)
                 got = ends(column(i, j, 0), column(i, j, 1), s, got)
@@ -452,10 +473,14 @@
     for p in range(2):
         side = 1 - p
         where = [late_from[2 * p + s] - CAP * side for s in range(2)]
-        ways = [jnp.where(flat < 64, *(edge_in[side, w, where[s]] for s in range(2)))[None] for w in range(2)]
-        got = [beyond(ways[1], ways[0], 8 * f) for f in range(4)]
-        got[H_] = got[H_] + beyond(in1[1, 8:9], in1[0, 8:9], 16 + 8 * p)
-        got = jnp.concatenate(got, axis=0)
+        ways = []
+        for w in range(2):
+            came = edge_in[side, w]
+            turned = pltpu.roll(came, 64, 1)
+            ways.append(jnp.where(flat < 64, *(jnp.where(where[s] == s, came, turned) for s in range(2))))
+        got = unshelved(ways[1], ways[0], 0)
+        got[H_] = got[H_] + beyond(in1[1, extra], in1[0, extra], 16 + 8 * p)
+        got = jnp.stack(got)
         for s in range(2):
             got = ends(late0[2 * p + s, :, 0, rows], late0[2 * p + s, :, tiles - 1, rows], s, got)
         late_strips[:, p, rows] = got
@@ -548,10 +573,10 @@
             pltpu.VMEM((nf, PAIRS, PITCH, LANES), f32),
             pltpu.VMEM((nf, PAIRS, PITCH, LANES), f32),
             pltpu.VMEM((nf, PAIRS, ny, LANES), f32),
-            pltpu.VMEM((2, 9, ny, LANES), f32),
-            pltpu.VMEM((2, 9, ny, LANES), f32),
-            pltpu.VMEM((2, 2, CAP, ny, LANES), f32),
-            pltpu.VMEM((2, 2, CAP, ny, LANES), f32),
+            pltpu.VMEM((2, 7, ny, LANES), f32),
+            pltpu.VMEM((2, 7, ny, LANES), f32),
+            pltpu.VMEM((2, 2, ny, LANES), f32),
+            pltpu.VMEM((2, 2, ny, LANES), f32),
             pltpu.SemaphoreType.DMA((5, tiles)),
             pltpu.SemaphoreType.DMA((2, tiles)),
             pltpu.SemaphoreType.DMA((2, tiles)),

time: 21.2 us -> 19.2 us (0.906)
  the two profiles are of different devices: /device:TPU:1 before, /device:TPU:7 now
where the time goes in v3:
time: 19.2 us
  Pallas kernels  19.2 us (100%)
    pallas_call x1, Pallas kernels, local(): pl.pallas_call(kernel, out_shape=handed, in_specs=[hbm] * 5, out_specs=[v...  16.8 us
    pallas_call x1, Pallas kernels, local(): pl.pallas_call(finish, out_shape=jax.ShapeDtypeStruct((pd, nf, ny, nx), f...  2.39 us

profile of v3, /device:TPU:7, one launch (start us, length us, event | category | flops | bytes accessed | tf_op | source)
XLA Modules:
  0.0 19.2 jit_solution(9746090372144781230)
XLA Ops:
  0.0 16.8 %resample_and_step.1 = (f32[32,4,4,16,128]{4,3,2,1,0:T(8,128)S(1)}, f32[4,4,4,32,128]{4,3,2,1,0:T(8,128)S(1)}, f32[4,2,32,128]{3,2,1,0:T(8,128)S(1)}, f32[5,16,1...) custom-call(s32[512]{0:T(512)} %anc_in.1, ...), custom_call_target="tpu_custom_call" | custom-call | tf_op jit(solution)/shard_map/resample_and_step/pallas_call | solution.py:556
  16.8 2.4 %finish.1 = f32[32,4,16,512]{3,2,1,0:T(8,128)} custom-call(f32[32,4,4,16,128]{4,3,2,1,0:T(8,128)S(1)} %get-tuple-element.12.made, f32[4,4,4,32,128]{4,3,2,1,0:T(8,128)S(1)} %get-tuple-element.13.late0, f32[4,2,32,128]{3,2,1,0:T(8,128)S(1)} %get-tuple-element.14.late_strips, f32[5,16,128]{2,1,0:T(8,128)S(1)} %get-tuple-element.15.gs, ...), custom_call_target="tpu_custom_call" | custom-call | tf_op jit(solution)/shard_map/finish/pallas_call | solution.py:593

commit v4 on v3

--- a/solution.py
+++ b/solution.py
@@ -18,7 +18,8 @@
 HALF = 8
 PAIRS = 7
 RUN = 8
-AHEAD = 4
+ROW = 8
+AHEAD = 3
 NEED = (EDGE, EDGE - 1, EDGE, EDGE - 3)
 SHELF = (0, 12, 6, 17)
 SLOT_LANES = 20
@@ -352,12 +353,17 @@
 
     def send():
         pl.semaphore_wait(barrier, 2 + jnp.where(k > 0, 3, 0) + jnp.where(k < doms - 1, 3, 0))
+        in_hurry = lax.rem(me, RUN) < RUN - 1
+        far_up = in_hurry & (lax.rem(k, ROW) == ROW - 1) & (k < doms - 1)
+        far_down = in_hurry & (lax.rem(k, ROW) == 0) & (k > 0)
+        send_particles(True, far_up)
+        send_particles(False, far_down)
         for rightward in (True, False):
             message(rightward).start()
             for up in (False, True):
                 edge_message(up, rightward).start()
-        send_particles(True, odd & (k < doms - 1))
-        send_particles(False, jnp.logical_not(odd) & (k > 0))
+        send_particles(True, odd & (k < doms - 1) & jnp.logical_not(far_up))
+        send_particles(False, jnp.logical_not(odd) & (k > 0) & jnp.logical_not(far_down))
         send_particles(True, jnp.logical_not(odd))
         send_particles(False, odd)
 

time: 19.2 us -> 19.3 us (level)
  no operation moved by 1% of the time
where the time goes in v4:
time: 19.3 us; the launch traced here: 19.2 us
  Pallas kernels  19.2 us (99%)
    pallas_call x1, Pallas kernels, local(): pl.pallas_call(kernel, out_shape=handed, in_specs=[hbm] * 5, out_specs=[v...  16.8 us
    pallas_call x1, Pallas kernels, local(): pl.pallas_call(finish, out_shape=jax.ShapeDtypeStruct((pd, nf, ny, nx), f...  2.39 us

profile of v4, /device:TPU:7, one launch (start us, length us, event | category | flops | bytes accessed | tf_op | source)
XLA Modules:
  0.0 19.2 jit_solution(6325100064029040197)
XLA Ops:
  0.0 16.8 %resample_and_step.1 = (f32[32,4,4,16,128]{4,3,2,1,0:T(8,128)S(1)}, f32[4,4,4,32,128]{4,3,2,1,0:T(8,128)S(1)}, f32[4,2,32,128]{3,2,1,0:T(8,128)S(1)}, f32[5,16,1...) custom-call(s32[512]{0:T(512)} %anc_in.1, ...), custom_call_target="tpu_custom_call" | custom-call | tf_op jit(solution)/shard_map/resample_and_step/pallas_call | solution.py:562
  16.9 2.4 %finish.1 = f32[32,4,16,512]{3,2,1,0:T(8,128)} custom-call(f32[32,4,4,16,128]{4,3,2,1,0:T(8,128)S(1)} %get-tuple-element.12.made, f32[4,4,4,32,128]{4,3,2,1,0:T(8,128)S(1)} %get-tuple-element.13.late0, f32[4,2,32,128]{3,2,1,0:T(8,128)S(1)} %get-tuple-element.14.late_strips, f32[5,16,128]{2,1,0:T(8,128)S(1)} %get-tuple-element.15.gs, ...), custom_call_target="tpu_custom_call" | custom-call | tf_op jit(solution)/shard_map/finish/pallas_call | solution.py:599

commit v5 on v3

--- a/solution.py
+++ b/solution.py
@@ -331,13 +331,13 @@
                 got = shelve(columns, rightward, 64 * t, got)
             edge_out[0 if up else 1, rightward] = got
 
-    def dom_copy(up, q):
+    def dom_copy(up, t):
         first, lands, to = (pd - CAP, 0, k + 1) if up else (0, CAP, k - 1)
         return pltpu.make_async_remote_copy(
-            src_ref=ens.at[first : first + CAP, :, :, tile(q)],
-            dst_ref=ext.at[lands : lands + CAP, :, q],
-            send_sem=dom_out_sem.at[int(up), q],
-            recv_sem=dom_in_sem.at[int(up), q],
+            src_ref=ens.at[first + t],
+            dst_ref=ext.at[lands + t],
+            send_sem=dom_out_sem.at[int(up), t],
+            recv_sem=dom_in_sem.at[int(up), t],
             device_id=(to, me),
             device_id_type=MESH,
         )
@@ -345,8 +345,8 @@
     def send_particles(up, on):
         @pl.when(on)
         def _():
-            for q in range(tiles):
-                dom_copy(up, q).start()
+            for t in range(CAP):
+                dom_copy(up, t).start()
 
     odd = lax.rem(k, 2) == 1
 
@@ -439,17 +439,19 @@
 
     @pl.when(k > 0)
     def _():
-        for q in range(tiles):
-            dom_copy(True, q).wait_recv()
+        for t in range(CAP):
+            dom_copy(True, t).wait_recv()
 
     @pl.when(k < doms - 1)
     def _():
-        for q in range(tiles):
-            dom_copy(False, q).wait_recv()
+        for t in range(CAP):
+            dom_copy(False, t).wait_recv()
 
     def own_particle(lands, j):
         for f in range(4):
-            ext[lands, f] = whole_rows(from_own(j), f, rows)
+            state = whole_rows(from_own(j), f, rows)
+            for q in range(tiles):
+                ext[lands, f, :, tile(q)] = state[q]
 
     @pl.when(k == 0)
     def _():
@@ -464,7 +466,7 @@
     late_from = [from_ext(j, j < CAP) for j in late]
     for t, j in enumerate(late):
         for f in range(4):
-            state = ext[late_from[t], f]
+            state = jnp.stack([ext[late_from[t], f, :, tile(q)] for q in range(tiles)])
             late0[t, f, :, rows] = 5.0 * (state + pv[j]) if f == H_ else state
 
     for side in range(2):
@@ -492,13 +494,13 @@
 
     @pl.when(k < doms - 1)
     def _():
-        for q in range(tiles):
-            dom_copy(True, q).wait_send()
+        for t in range(CAP):
+            dom_copy(True, t).wait_send()
 
     @pl.when(k > 0)
     def _():
-        for q in range(tiles):
-            dom_copy(False, q).wait_send()
+        for t in range(CAP):
+            dom_copy(False, t).wait_send()
 
 
 def finish(made, late0, late_strips, gs, gw, gd, go, out, late_out, s1, s2, b1, b2, b3, sem):
@@ -562,7 +564,7 @@
             pltpu.SMEM(ancestors.shape, jnp.int32),
             pltpu.VMEM((pd, nf, 2, PITCH, LANES), f32),
             pltpu.VMEM((pd, nf, tiles - 2, PITCH, LANES), f32),
-            pltpu.VMEM((2 * CAP, nf, tiles, ny, LANES), f32),
+            pltpu.VMEM((2 * CAP, nf, ny, nx), f32),
             pltpu.VMEM((pd, tiles, PITCH, LANES), f32),
             pltpu.VMEM((pd, tiles, ny, LANES), f32),
             pltpu.VMEM((tiles, ny, LANES), jnp.int32),
@@ -578,8 +580,8 @@
             pltpu.VMEM((2, 2, ny, LANES), f32),
             pltpu.VMEM((2, 2, ny, LANES), f32),
             pltpu.SemaphoreType.DMA((5, tiles)),
-            pltpu.SemaphoreType.DMA((2, tiles)),
-            pltpu.SemaphoreType.DMA((2, tiles)),
+            pltpu.SemaphoreType.DMA((2, CAP)),
+            pltpu.SemaphoreType.DMA((2, CAP)),
             pltpu.SemaphoreType.DMA((2,)),
             pltpu.SemaphoreType.DMA((2,)),
             pltpu.SemaphoreType.DMA((2, 2)),

time: 19.2 us -> 19.2 us (level)
  no operation moved by 1% of the time
where the time goes in v5:
time: 19.2 us; the launch traced here: 19.1 us
  Pallas kernels  19.1 us (99%)
    pallas_call x1, Pallas kernels, local(): pl.pallas_call(kernel, out_shape=handed, in_specs=[hbm] * 5, out_specs=[v...  16.7 us
    pallas_call x1, Pallas kernels, local(): pl.pallas_call(finish, out_shape=jax.ShapeDtypeStruct((pd, nf, ny, nx), f...  2.39 us

profile of v5, /device:TPU:7, one launch (start us, length us, event | category | flops | bytes accessed | tf_op | source)
XLA Modules:
  0.0 19.1 jit_solution(18108346486846554555)
XLA Ops:
  0.0 16.7 %resample_and_step.1 = (f32[32,4,4,16,128]{4,3,2,1,0:T(8,128)S(1)}, f32[4,4,4,32,128]{4,3,2,1,0:T(8,128)S(1)}, f32[4,2,32,128]{3,2,1,0:T(8,128)S(1)}, f32[5,16,1...) custom-call(s32[512]{0:T(512)} %anc_in.1, ...), custom_call_target="tpu_custom_call" | custom-call | tf_op jit(solution)/shard_map/resample_and_step/pallas_call | solution.py:558
  16.7 2.4 %finish.1 = f32[32,4,16,512]{3,2,1,0:T(8,128)} custom-call(f32[32,4,4,16,128]{4,3,2,1,0:T(8,128)S(1)} %get-tuple-element.12.made, f32[4,4,4,32,128]{4,3,2,1,0:T(8,128)S(1)} %get-tuple-element.13.late0, f32[4,2,32,128]{3,2,1,0:T(8,128)S(1)} %get-tuple-element.14.late_strips, f32[5,16,128]{2,1,0:T(8,128)S(1)} %get-tuple-element.15.gs, ...), custom_call_target="tpu_custom_call" | custom-call | tf_op jit(solution)/shard_map/finish/pallas_call | solution.py:595

commit v6 on v5

--- a/solution.py
+++ b/solution.py
@@ -18,7 +18,8 @@
 HALF = 8
 PAIRS = 7
 RUN = 8
-AHEAD = 4
+LAGS = 4
+AHEAD = (6, 3)
 NEED = (EDGE, EDGE - 1, EDGE, EDGE - 3)
 SHELF = (0, 12, 6, 17)
 SLOT_LANES = 20
@@ -182,7 +183,7 @@
 def kernel(
     anc_in, ens, pert, lev, obs, out, late0, late_strips, gs, gw, gd, go,
     anc, ends_of, inner, ext, h0, pv, lv, ov, s1, s2, b0, b1, b2, b3, out1, in1, edge_out, edge_in,
-    in_sem, dom_out_sem, dom_in_sem, msg_out_sem, msg_in_sem, edge_out_sem, edge_in_sem,
+    in_sem, dom_out_sem, dom_in_sem, msg_out_sem, msg_in_sem, edge_out_sem, edge_in_sem, entered,
 ):
     pd = ens.shape[0]
     ny = ens.shape[2]
@@ -195,19 +196,37 @@
 
     barrier = pltpu.get_barrier_semaphore()
 
-    def greet(dom, *spaces_there):
-        for space in spaces_there:
-            pl.semaphore_signal(barrier, inc=1, device_id=(dom, space), device_id_type=MESH)
-
-    greet(k, prev_space, next_space)
+    def signal(semaphore, dom, space):
+        pl.semaphore_signal(semaphore, inc=1, device_id=(dom, space), device_id_type=MESH)
+
+    def signal_side(semaphore, rightward):
+        space = next_space if rightward else prev_space
+        signal(semaphore, k, space)
+
+        @pl.when(k > 0)
+        def _():
+            signal(semaphore, k - 1, space)
+
+        @pl.when(k < doms - 1)
+        def _():
+            signal(semaphore, k + 1, space)
+
+    place = lax.rem(me, RUN)
+    late_side = (place == 0, place < LAGS)
+    ahead_side = ((place > 0) & (place <= LAGS), place == RUN - 1)
+    dom_peers = jnp.where(k > 0, 1, 0) + jnp.where(k < doms - 1, 1, 0)
+    side_peers = 1 + dom_peers
 
     @pl.when(k > 0)
     def _():
-        greet(k - 1, me, prev_space, next_space)
+        signal(barrier, k - 1, me)
 
     @pl.when(k < doms - 1)
     def _():
-        greet(k + 1, me, prev_space, next_space)
+        signal(barrier, k + 1, me)
+
+    for side in range(2):
+        pl.when(jnp.logical_not(ahead_side[side]))(functools.partial(signal_side, barrier, side))
 
     def tile(q):
         return pl.ds(q * LANES, LANES)
@@ -350,19 +369,26 @@
 
     odd = lax.rem(k, 2) == 1
 
-    def send():
-        pl.semaphore_wait(barrier, 2 + jnp.where(k > 0, 3, 0) + jnp.where(k < doms - 1, 3, 0))
-        for rightward in (True, False):
-            message(rightward).start()
-            for up in (False, True):
-                edge_message(up, rightward).start()
-        send_particles(True, odd & (k < doms - 1))
-        send_particles(False, jnp.logical_not(odd) & (k > 0))
-        send_particles(True, jnp.logical_not(odd))
-        send_particles(False, odd)
-
-    ahead = lax.rem(me, RUN) == 0
-    pl.when(jnp.logical_not(ahead))(send)
+    def send_side(rightward):
+        message(rightward).start()
+        for up in (False, True):
+            edge_message(up, rightward).start()
+
+    pl.semaphore_wait(
+        barrier, dom_peers + sum(jnp.where(late_side[side], 0, side_peers) for side in range(2))
+    )
+    for side in (1, 0):
+        pl.when(ahead_side[side])(functools.partial(signal_side, entered.at[1 - side], side))
+    for side in (1, 0):
+        pl.when(jnp.logical_not(late_side[side]))(functools.partial(send_side, side))
+    send_particles(True, odd & (k < doms - 1))
+    send_particles(False, jnp.logical_not(odd) & (k > 0))
+    send_particles(True, jnp.logical_not(odd))
+    send_particles(False, odd)
+
+    def send_late(side):
+        pl.semaphore_wait(entered.at[side], side_peers)
+        send_side(side)
 
     for copy in needed_next:
         copy.wait()
@@ -381,7 +407,8 @@
 
     @pl.loop(0, early // UNIT)
     def _(u):
-        pl.when(ahead & (u == AHEAD))(send)
+        for side in range(2):
+            pl.when(late_side[side] & (u == AHEAD[side]))(functools.partial(send_late, side))
         slots = [CAP + u * UNIT + s for s in range(UNIT)]
         where = [from_own(j) for j in slots]
 
@@ -586,6 +613,7 @@
             pltpu.SemaphoreType.DMA((2,)),
             pltpu.SemaphoreType.DMA((2, 2)),
             pltpu.SemaphoreType.DMA((2, 2)),
+            pltpu.SemaphoreType.REGULAR((2,)),
         ],
         compiler_params=pltpu.CompilerParams(
             collective_id=0, has_side_effects=True, vmem_limit_bytes=40 * 1024 * 1024

time: 19.2 us -> 18.3 us (0.953)
  Pallas kernels: 19.1 us -> 18.2 us
    pallas_call x1, Pallas kernels: 16.7 us -> 15.8 us  [local(): pl.pallas_call(kernel, out_shape=handed, in_specs=[hbm] * 5, out_specs=[v...]
where the time goes in v6:
time: 18.3 us; the launch traced here: 18.2 us
  Pallas kernels  18.2 us (99%)
    pallas_call x1, Pallas kernels, local(): pl.pallas_call(kernel, out_shape=handed, in_specs=[hbm] * 5, out_specs=[v...  15.8 us
    pallas_call x1, Pallas kernels, local(): pl.pallas_call(finish, out_shape=jax.ShapeDtypeStruct((pd, nf, ny, nx), f...  2.37 us

profile of v6, /device:TPU:7, one launch (start us, length us, event | category | flops | bytes accessed | tf_op | source)
XLA Modules:
  0.0 18.2 jit_solution(1483390991644034525)
XLA Ops:
  0.0 15.8 %resample_and_step.1 = (f32[32,4,4,16,128]{4,3,2,1,0:T(8,128)S(1)}, f32[4,4,4,32,128]{4,3,2,1,0:T(8,128)S(1)}, f32[4,2,32,128]{3,2,1,0:T(8,128)S(1)}, f32[5,16,1...) custom-call(s32[512]{0:T(512)} %anc_in.1, ...), custom_call_target="tpu_custom_call" | custom-call | tf_op jit(solution)/shard_map/resample_and_step/pallas_call | solution.py:585
  15.8 2.4 %finish.1 = f32[32,4,16,512]{3,2,1,0:T(8,128)} custom-call(f32[32,4,4,16,128]{4,3,2,1,0:T(8,128)S(1)} %get-tuple-element.12.made, f32[4,4,4,32,128]{4,3,2,1,0:T(8,128)S(1)} %get-tuple-element.13.late0, f32[4,2,32,128]{3,2,1,0:T(8,128)S(1)} %get-tuple-element.14.late_strips, f32[5,16,128]{2,1,0:T(8,128)S(1)} %get-tuple-element.15.gs, ...), custom_call_target="tpu_custom_call" | custom-call | tf_op jit(solution)/shard_map/finish/pallas_call | solution.py:623

commit v7 on v6

--- a/solution.py
+++ b/solution.py
@@ -16,6 +16,7 @@
 PITCH = 32
 UNIT = 4
 HALF = 8
+ROW = 8
 PAIRS = 7
 RUN = 8
 LAGS = 4
@@ -172,6 +173,12 @@
         pltpu.store(out.at[j, :, final], at_right, mask=lane >= LANES - EDGE)
 
 
+def late_soon(k, me, doms):
+    inner_end = (lax.rem(k, ROW) == ROW - 1) & (k < doms - 1)
+    inner_start = (lax.rem(k, ROW) == 0) & (k > 0)
+    return (lax.rem(me, RUN) == 0) & jnp.logical_not(inner_end | inner_start)
+
+
 def clear_rows(ref, ny):
     @pl.loop(0, ref.shape[0])
     def _(i):
@@ -181,7 +188,7 @@
 
 
 def kernel(
-    anc_in, ens, pert, lev, obs, out, late0, late_strips, gs, gw, gd, go,
+    anc_in, ens, pert, lev, obs, out, late_made, late0, late_strips, gs, gw, gd, go,
     anc, ends_of, inner, ext, h0, pv, lv, ov, s1, s2, b0, b1, b2, b3, out1, in1, edge_out, edge_in,
     in_sem, dom_out_sem, dom_in_sem, msg_out_sem, msg_in_sem, edge_out_sem, edge_in_sem, entered,
 ):
@@ -245,6 +252,35 @@
 
     for ref in (ends_of, inner, h0, late0, s1, s2, b0, b1, b2, late_strips):
         clear_rows(ref, ny)
+
+    def dom_copy(up, t):
+        first, lands, to = (pd - CAP, 0, k + 1) if up else (0, CAP, k - 1)
+        return pltpu.make_async_remote_copy(
+            src_ref=ens.at[first + t],
+            dst_ref=ext.at[lands + t],
+            send_sem=dom_out_sem.at[int(up), t],
+            recv_sem=dom_in_sem.at[int(up), t],
+            device_id=(to, me),
+            device_id_type=MESH,
+        )
+
+    def send_particles(up, on):
+        @pl.when(on)
+        def _():
+            for t in range(CAP):
+                dom_copy(up, t).start()
+
+    pl.semaphore_wait(
+        barrier, dom_peers + sum(jnp.where(late_side[side], 0, side_peers) for side in range(2))
+    )
+    for side in (1, 0):
+        pl.when(ahead_side[side])(functools.partial(signal_side, entered.at[1 - side], side))
+    odd = lax.rem(k, 2) == 1
+    row_end, row_start = lax.rem(k, ROW) == ROW - 1, lax.rem(k, ROW) == 0
+    far_up = row_end & (k < doms - 1) & (place < RUN - 1)
+    far_down = row_start & (k > 0) & (place < RUN - 1)
+    send_particles(True, far_up)
+    send_particles(False, far_down)
 
     for copy in needed_first:
         copy.wait()
@@ -350,39 +386,15 @@
                 got = shelve(columns, rightward, 64 * t, got)
             edge_out[0 if up else 1, rightward] = got
 
-    def dom_copy(up, t):
-        first, lands, to = (pd - CAP, 0, k + 1) if up else (0, CAP, k - 1)
-        return pltpu.make_async_remote_copy(
-            src_ref=ens.at[first + t],
-            dst_ref=ext.at[lands + t],
-            send_sem=dom_out_sem.at[int(up), t],
-            recv_sem=dom_in_sem.at[int(up), t],
-            device_id=(to, me),
-            device_id_type=MESH,
-        )
-
-    def send_particles(up, on):
-        @pl.when(on)
-        def _():
-            for t in range(CAP):
-                dom_copy(up, t).start()
-
-    odd = lax.rem(k, 2) == 1
-
     def send_side(rightward):
         message(rightward).start()
         for up in (False, True):
             edge_message(up, rightward).start()
 
-    pl.semaphore_wait(
-        barrier, dom_peers + sum(jnp.where(late_side[side], 0, side_peers) for side in range(2))
-    )
-    for side in (1, 0):
-        pl.when(ahead_side[side])(functools.partial(signal_side, entered.at[1 - side], side))
     for side in (1, 0):
         pl.when(jnp.logical_not(late_side[side]))(functools.partial(send_side, side))
-    send_particles(True, odd & (k < doms - 1))
-    send_particles(False, jnp.logical_not(odd) & (k > 0))
+    send_particles(True, odd & (k < doms - 1) & jnp.logical_not(far_up))
+    send_particles(False, jnp.logical_not(odd) & (k > 0) & jnp.logical_not(far_down))
     send_particles(True, jnp.logical_not(odd))
     send_particles(False, odd)
 
@@ -420,6 +432,53 @@
             out[slots[i], field, :, pl.ds(y0, HALF)] = value
 
         all_steps(first, s1, s2, row_ground(gw, gd, go), keep, True, ny, slot_parts())
+
+    late_from = [from_ext(j, j < CAP) for j in late]
+    soon = late_soon(k, me, doms)
+
+    def take_late():
+        @pl.when(k > 0)
+        def _():
+            for t in range(CAP):
+                dom_copy(True, t).wait_recv()
+
+        @pl.when(k < doms - 1)
+        def _():
+            for t in range(CAP):
+                dom_copy(False, t).wait_recv()
+
+        def own_particle(lands, j):
+            for f in range(4):
+                state = whole_rows(from_own(j), f, rows)
+                for q in range(tiles):
+                    ext[lands, f, :, tile(q)] = state[q]
+
+        @pl.when(k == 0)
+        def _():
+            for s in range(CAP):
+                own_particle(s, s)
+
+        @pl.when(k == doms - 1)
+        def _():
+            for s in range(CAP, 2 * CAP):
+                own_particle(s, pd - 2 * CAP + s)
+
+        for t, j in enumerate(late):
+            for f in range(4):
+                state = jnp.stack([ext[late_from[t], f, :, tile(q)] for q in range(tiles)])
+                late0[t, f, :, rows] = 5.0 * (state + pv[j]) if f == H_ else state
+
+    @pl.when(soon)
+    def _():
+        take_late()
+
+        def keep(i, field, y0, value):
+            late_made[i, field, :, pl.ds(y0, HALF)] = value
+
+        all_steps(
+            lambda i, field, y0, up: late0[i, field, :, pl.ds(TOP + y0 + up, HALF)],
+            s1, s2, row_ground(gw, gd, go), keep, True, ny, slot_parts(),
+        )
 
     for rightward in (False, True):
         message(rightward).wait_recv()
@@ -464,37 +523,7 @@
         for p in range(PAIRS):
             put_strips(b3, p, slots[p], out)
 
-    @pl.when(k > 0)
-    def _():
-        for t in range(CAP):
-            dom_copy(True, t).wait_recv()
-
-    @pl.when(k < doms - 1)
-    def _():
-        for t in range(CAP):
-            dom_copy(False, t).wait_recv()
-
-    def own_particle(lands, j):
-        for f in range(4):
-            state = whole_rows(from_own(j), f, rows)
-            for q in range(tiles):
-                ext[lands, f, :, tile(q)] = state[q]
-
-    @pl.when(k == 0)
-    def _():
-        for s in range(CAP):
-            own_particle(s, s)
-
-    @pl.when(k == doms - 1)
-    def _():
-        for s in range(CAP, 2 * CAP):
-            own_particle(s, pd - 2 * CAP + s)
-
-    late_from = [from_ext(j, j < CAP) for j in late]
-    for t, j in enumerate(late):
-        for f in range(4):
-            state = jnp.stack([ext[late_from[t], f, :, tile(q)] for q in range(tiles)])
-            late0[t, f, :, rows] = 5.0 * (state + pv[j]) if f == H_ else state
+    pl.when(jnp.logical_not(soon))(take_late)
 
     for side in range(2):
         for rightward in (False, True):
@@ -530,7 +559,7 @@
             dom_copy(False, t).wait_send()
 
 
-def finish(made, late0, late_strips, gs, gw, gd, go, out, late_out, s1, s2, b1, b2, b3, sem):
+def finish(made, late_made, late0, late_strips, gs, gw, gd, go, out, late_out, s1, s2, b1, b2, b3, sem):
     pd, nf, tiles, ny, _ = made.shape
 
     def tile(q):
@@ -545,13 +574,22 @@
     for ref in (s1, s2, b1, b2):
         clear_rows(ref, ny)
 
-    def keep(i, field, y0, value):
-        late_out[i, field, :, pl.ds(y0, HALF)] = value
-
-    all_steps(
-        lambda i, field, y0, up: late0[i, field, :, pl.ds(TOP + y0 + up, HALF)],
-        s1, s2, row_ground(gw, gd, go), keep, True, ny, slot_parts(),
-    )
+    soon = late_soon(lax.axis_index("dom"), lax.axis_index("space"), lax.axis_size("dom"))
+
+    @pl.when(soon)
+    def _():
+        late_out[...] = late_made[...]
+
+    @pl.when(jnp.logical_not(soon))
+    def _():
+        def keep(i, field, y0, value):
+            late_out[i, field, :, pl.ds(y0, HALF)] = value
+
+        all_steps(
+            lambda i, field, y0, up: late0[i, field, :, pl.ds(TOP + y0 + up, HALF)],
+            s1, s2, row_ground(gw, gd, go), keep, True, ny, slot_parts(),
+        )
+
     step_strips(late_strips, b1, b2, b3, gs, [slice(0, CAP)], ny)
     for p in range(2):
         put_strips(b3, p, [2 * p, 2 * p + 1], late_out)
@@ -575,6 +613,7 @@
     state = (UNIT, nf, tiles, PITCH, LANES)
     handed = [
         pltpu.VMEM((pd, nf, tiles, ny, LANES), f32),
+        pltpu.VMEM((UNIT, nf, tiles, ny, LANES), f32),
         pltpu.VMEM(state, f32),
         pltpu.VMEM((nf, CAP, PITCH, LANES), f32),
         pltpu.VMEM((5, ny, LANES), f32),

time: 18.3 us -> 18.6 us (1.016)
  Pallas kernels: 18.2 us -> 18.4 us
    pallas_call x1, Pallas kernels: 2.37 us -> 2.58 us  [local(): pl.pallas_call(finish, out_shape=jax.ShapeDtypeStruct((pd, nf, ny, nx), f...]
where the time goes in v7:
time: 18.6 us; the launch traced here: 18.4 us
  Pallas kernels  18.4 us (99%)
    pallas_call x1, Pallas kernels, local(): pl.pallas_call(kernel, out_shape=handed, in_specs=[hbm] * 5, out_specs=[v...  15.8 us
    pallas_call x1, Pallas kernels, local(): pl.pallas_call(finish, out_shape=jax.ShapeDtypeStruct((pd, nf, ny, nx), f...  2.58 us

profile of v7, /device:TPU:7, one launch (start us, length us, event | category | flops | bytes accessed | tf_op | source)
XLA Modules:
  0.0 18.4 jit_solution(1505272862471104868)
XLA Ops:
  0.0 15.8 %resample_and_step.1 = (f32[32,4,4,16,128]{4,3,2,1,0:T(8,128)S(1)}, f32[4,4,4,16,128]{4,3,2,1,0:T(8,128)S(1)}, f32[4,4,4,32,128]{4,3,2,1,0:T(8,128)S(1)}, f32[4,...) custom-call(s32[512]{0:T(512)} %anc_in.1, ...), custom_call_target="tpu_custom_call" | custom-call | tf_op jit(solution)/shard_map/resample_and_step/pallas_call | solution.py:624
  15.8 2.6 %finish.1 = f32[32,4,16,512]{3,2,1,0:T(8,128)} custom-call(f32[32,4,4,16,128]{4,3,2,1,0:T(8,128)S(1)} %get-tuple-element.13.made, f32[4,4,4,16,128]{4,3,2,1,0:T(8,128)S(1)} %get-tuple-element.14.late_made, f32[4,4,4,32,128]{4,3,2,1,0:T(8,128)S(1)} %get-tuple-element.15.late0, f32[4,2,32,128]{3,2,1,0:T(8,128)S(1)} %get-tuple-element.16.late_strips, ...), custom_call_target="tpu_custom_call" | custom-call | tf_op jit(solution)/shard_map/finish/pallas_call | solution.py:662

commit v8 on v7

--- a/solution.py
+++ b/solution.py
@@ -20,7 +20,7 @@
 PAIRS = 7
 RUN = 8
 LAGS = 4
-AHEAD = (6, 3)
+AHEAD = (5, 2)
 NEED = (EDGE, EDGE - 1, EDGE, EDGE - 3)
 SHELF = (0, 12, 6, 17)
 SLOT_LANES = 20
@@ -279,8 +279,6 @@
     row_end, row_start = lax.rem(k, ROW) == ROW - 1, lax.rem(k, ROW) == 0
     far_up = row_end & (k < doms - 1) & (place < RUN - 1)
     far_down = row_start & (k > 0) & (place < RUN - 1)
-    send_particles(True, far_up)
-    send_particles(False, far_down)
 
     for copy in needed_first:
         copy.wait()
@@ -353,23 +351,21 @@
 
     shelves = -(-PAIRS // TRIPLE)
 
-    @pl.loop(0, early // (2 * PAIRS))
-    def _(m):
-        for r in range(shelves):
-            packed = [jnp.zeros((ny, LANES), jnp.float32)] * 2
-            for p in range(TRIPLE * r, min(PAIRS, TRIPLE * r + TRIPLE)):
-                for s in range(2):
-                    j = CAP + 2 * (PAIRS * m + p) + s
-                    i = from_own(j)
-                    for side in range(2):
+    def pack(side):
+        @pl.loop(0, early // (2 * PAIRS))
+        def _(m):
+            for r in range(shelves):
+                packed = jnp.zeros((ny, LANES), jnp.float32)
+                for p in range(TRIPLE * r, min(PAIRS, TRIPLE * r + TRIPLE)):
+                    for s in range(2):
+                        j = CAP + 2 * (PAIRS * m + p) + s
                         at = 64 * s + SLOT_LANES * (p - TRIPLE * r)
-                        packed[side] = shelve(column(i, j, side), side, at, packed[side])
-            for side in range(2):
-                out1[side, shelves * m + r] = packed[side]
+                        packed = shelve(column(from_own(j), j, side), side, at, packed)
+                out1[side, shelves * m + r] = packed
 
     extra = shelves * (early // (2 * PAIRS))
     late = [pd - 2, pd - 1, 0, 1]
-    for rightward in range(2):
+    def pack_extra(rightward):
         q, end = (tiles - 1, EDGE) if rightward else (0, 0)
         got = jnp.zeros((ny, LANES), jnp.float32)
         parts = [(lv[q].astype(jnp.float32), at) for at in (0, 64)] + [(ov[q], at) for at in (8, 72)]
@@ -377,6 +373,8 @@
         for part, at in parts:
             got = jnp.where((flat >= at) & (flat < at + EDGE), pltpu.roll(part, at + end, 1), got)
         out1[rightward, extra] = got
+
+    for rightward in range(2):
         for up in (True, False):
             got = jnp.zeros((ny, LANES), jnp.float32)
             for t in range(CAP):
@@ -386,13 +384,21 @@
                 got = shelve(columns, rightward, 64 * t, got)
             edge_out[0 if up else 1, rightward] = got
 
-    def send_side(rightward):
-        message(rightward).start()
+    def send_edges(rightward):
         for up in (False, True):
             edge_message(up, rightward).start()
 
+    def send_message(rightward):
+        message(rightward).start()
+
     for side in (1, 0):
-        pl.when(jnp.logical_not(late_side[side]))(functools.partial(send_side, side))
+        pl.when(jnp.logical_not(late_side[side]))(functools.partial(send_edges, side))
+    send_particles(True, far_up)
+    send_particles(False, far_down)
+    for side in (1, 0):
+        pack(side)
+        pack_extra(side)
+        pl.when(jnp.logical_not(late_side[side]))(functools.partial(send_message, side))
     send_particles(True, odd & (k < doms - 1) & jnp.logical_not(far_up))
     send_particles(False, jnp.logical_not(odd) & (k > 0) & jnp.logical_not(far_down))
     send_particles(True, jnp.logical_not(odd))
@@ -400,7 +406,8 @@
 
     def send_late(side):
         pl.semaphore_wait(entered.at[side], side_peers)
-        send_side(side)
+        send_edges(side)
+        send_message(side)
 
     for copy in needed_next:
         copy.wait()

time: 18.6 us -> 19.4 us (1.043)
  Pallas kernels: 18.4 us -> 19.3 us
    pallas_call x1, Pallas kernels: 15.8 us -> 16.8 us  [local(): pl.pallas_call(kernel, out_shape=handed, in_specs=[hbm] * 5, out_specs=[v...]
where the time goes in v8:
time: 19.4 us
  Pallas kernels  19.3 us (99%)
    pallas_call x1, Pallas kernels, local(): pl.pallas_call(kernel, out_shape=handed, in_specs=[hbm] * 5, out_specs=[v...  16.8 us
    pallas_call x1, Pallas kernels, local(): pl.pallas_call(finish, out_shape=jax.ShapeDtypeStruct((pd, nf, ny, nx), f...  2.59 us

profile of v8, /device:TPU:7, one launch (start us, length us, event | category | flops | bytes accessed | tf_op | source)
XLA Modules:
  0.0 19.4 jit_solution(16216262709882276839)
XLA Ops:
  0.0 16.8 %resample_and_step.1 = (f32[32,4,4,16,128]{4,3,2,1,0:T(8,128)S(1)}, f32[4,4,4,16,128]{4,3,2,1,0:T(8,128)S(1)}, f32[4,4,4,32,128]{4,3,2,1,0:T(8,128)S(1)}, f32[4,...) custom-call(s32[512]{0:T(512)} %anc_in.1, ...), custom_call_target="tpu_custom_call" | custom-call | tf_op jit(solution)/shard_map/resample_and_step/pallas_call | solution.py:631
  16.8 2.6 %finish.1 = f32[32,4,16,512]{3,2,1,0:T(8,128)} custom-call(f32[32,4,4,16,128]{4,3,2,1,0:T(8,128)S(1)} %get-tuple-element.13.made, f32[4,4,4,16,128]{4,3,2,1,0:T(8,128)S(1)} %get-tuple-element.14.late_made, f32[4,4,4,32,128]{4,3,2,1,0:T(8,128)S(1)} %get-tuple-element.15.late0, f32[4,2,32,128]{3,2,1,0:T(8,128)S(1)} %get-tuple-element.16.late_strips, ...), custom_call_target="tpu_custom_call" | custom-call | tf_op jit(solution)/shard_map/finish/pallas_call | solution.py:669

commit v9 on v6

--- a/solution.py
+++ b/solution.py
@@ -19,7 +19,7 @@
 PAIRS = 7
 RUN = 8
 LAGS = 4
-AHEAD = (6, 3)
+AHEAD = (5, 2)
 NEED = (EDGE, EDGE - 1, EDGE, EDGE - 3)
 SHELF = (0, 12, 6, 17)
 SLOT_LANES = 20

time: 18.3 us -> 19.2 us (1.049)
  Pallas kernels: 18.2 us -> 19.1 us
    pallas_call x1, Pallas kernels: 15.8 us -> 16.8 us  [local(): pl.pallas_call(kernel, out_shape=handed, in_specs=[hbm] * 5, out_specs=[v...]
where the time goes in v9:
time: 19.2 us; the launch traced here: 19.1 us
  Pallas kernels  19.1 us (99%)
    pallas_call x1, Pallas kernels, local(): pl.pallas_call(kernel, out_shape=handed, in_specs=[hbm] * 5, out_specs=[v...  16.8 us
    pallas_call x1, Pallas kernels, local(): pl.pallas_call(finish, out_shape=jax.ShapeDtypeStruct((pd, nf, ny, nx), f...  2.37 us

profile of v9, /device:TPU:7, one launch (start us, length us, event | category | flops | bytes accessed | tf_op | source)
XLA Modules:
  0.0 19.1 jit_solution(16579374134923392933)
XLA Ops:
  0.0 16.8 %resample_and_step.1 = (f32[32,4,4,16,128]{4,3,2,1,0:T(8,128)S(1)}, f32[4,4,4,32,128]{4,3,2,1,0:T(8,128)S(1)}, f32[4,2,32,128]{3,2,1,0:T(8,128)S(1)}, f32[5,16,1...) custom-call(s32[512]{0:T(512)} %anc_in.1, ...), custom_call_target="tpu_custom_call" | custom-call | tf_op jit(solution)/shard_map/resample_and_step/pallas_call | solution.py:585
  16.8 2.4 %finish.1 = f32[32,4,16,512]{3,2,1,0:T(8,128)} custom-call(f32[32,4,4,16,128]{4,3,2,1,0:T(8,128)S(1)} %get-tuple-element.12.made, f32[4,4,4,32,128]{4,3,2,1,0:T(8,128)S(1)} %get-tuple-element.13.late0, f32[4,2,32,128]{3,2,1,0:T(8,128)S(1)} %get-tuple-element.14.late_strips, f32[5,16,128]{2,1,0:T(8,128)S(1)} %get-tuple-element.15.gs, ...), custom_call_target="tpu_custom_call" | custom-call | tf_op jit(solution)/shard_map/finish/pallas_call | solution.py:623
